TPU v7x, 128 devices: a whole 4x4x4 slice. The times are simulated.
128 devices in a mesh: clip: 4 (over y_hi, core), tm: 32 (over x, z, y_lo).
Axes of the slice: x: 4, y: 4 (y_hi: 2, y_lo: 2; y = y_hi * 2 + y_lo), z: 4, core: 2. Of those that a mesh axis runs over, the one named last changes fastest.
Arguments:
- half_one: bfloat16 [4, 32, 14, 14, 768], P('clip', 'tm'), may hold values from -6 to 6
- half_two: bfloat16 [4, 32, 14, 14, 768], P('clip', 'tm'), may hold values from -6 to 6
- grad_one: bfloat16 [4, 32, 14, 14, 768], P('clip', 'tm'), may hold values from -6 to 6
- grad_two: bfloat16 [4, 32, 14, 14, 768], P('clip', 'tm'), may hold values from -12 to 12
- norm_gain: float32 [2, 768], replicated, may hold values from 0.1 to 1.9
- attn_weight: bfloat16 [4, 768, 768], replicated, may hold values from -0.21875 to 0.21875
- mlp_weight: bfloat16 [2, 3072, 768], replicated, may hold values from -0.15625 to 0.15625
- pool_kernel: float32 [3, 4, 4, 1536], replicated, may hold values from -0.875 to 0.875
Outputs:
- input_one: bfloat16 [4, 32, 14, 14, 768], P('clip', 'tm')
- input_two: bfloat16 [4, 32, 14, 14, 768], P('clip', 'tm')
- input_grad_one: bfloat16 [4, 32, 14, 14, 768], P('clip', 'tm')
- input_grad_two: bfloat16 [4, 32, 14, 14, 768], P('clip', 'tm')
- attn_grad: float32 [4, 768, 768], P(None, None, ('clip', 'tm'))
- mlp_grad: float32 [2, 3072, 768], P(None, None, ('clip', 'tm'))
- kernel_grad: float32 [3, 4, 4, 1536], P(None, None, None, ('clip', 'tm'))
- gain_grad: float32 [2, 768], P(None, ('clip', 'tm'))
All inputs are finite; a program needn't handle non-finite values.
Results may differ from a plain program's by a relative error of at most 0.025.
Values may be sent and summed in bfloat16 or wider, within the bound.
A program may use at most 192 MiB of HBM per device.

v0:
```python
from functools import partial

import jax
import jax.numpy as jnp
from jax import lax
from jax.sharding import PartitionSpec as P

HEAD_DIM = 64


def extended(block, sides, width):
    for axis, dim in sides:
        count = lax.axis_size(axis)
        forward = [(i, i + 1) for i in range(count - 1)]
        backward = [(target, source) for source, target in forward]
        low = lax.ppermute(
            lax.slice_in_dim(block, block.shape[dim] - width, None, axis=dim), axis, forward
        )
        high = lax.ppermute(lax.slice_in_dim(block, 0, width, axis=dim), axis, backward)
        block = jnp.concatenate([low, block, high], axis=dim)
    return block


def normalize(values, gain):
    centre = jnp.mean(values, axis=-1, keepdims=True)
    centred = values - centre
    spread = jnp.mean(centred * centred, axis=-1, keepdims=True)
    return centred * lax.rsqrt(spread + 1e-05) * gain


def pool_frames(frames_in, kernel):
    length = frames_in.shape[1] - 2
    padded = jnp.pad(frames_in, ((0, 0), (0, 0), (1, 1), (1, 1), (0, 0)))
    blocks = padded.reshape(frames_in.shape[0], length + 2, 4, 4, 4, 4, frames_in.shape[-1])
    result = jnp.zeros((frames_in.shape[0], length, 4, 4, frames_in.shape[-1]), jnp.float32)
    for offset in range(3):
        result = result + jnp.einsum(
            "ctaibje,ije->ctabe", blocks[:, offset : offset + length], kernel[offset]
        )
    return result.reshape(frames_in.shape[0], length * 16, frames_in.shape[-1])


def pool_widened(frames_in, kernel):
    widened = jnp.pad(frames_in, ((0, 0), (2, 2), (0, 0), (0, 0), (0, 0)))
    return pool_frames(widened, kernel)


def shards(half_one, half_two, grad_one, grad_two, norm_gain, attn_weight, mlp_weight, pool_kernel):
    clips, frame_count, grid_rows, grid_cols, width = half_one.shape
    score_scale = HEAD_DIM ** (-0.5)
    heads = width // HEAD_DIM
    rows = clips * frame_count * grid_rows * grid_cols
    queries = frame_count * grid_rows * grid_cols
    one_flat = half_one.reshape(rows, width)
    two_flat = half_two.reshape(rows, width)
    cot_one_flat = grad_one.reshape(rows, width)
    cot_two_flat = grad_two.reshape(rows, width)
    contract_last = (((1,), (1,)), ((), ()))
    contract_first = (((0,), (0,)), ((), ()))
    normed_one = normalize(one_flat.astype(jnp.float32), norm_gain[0]).astype(jnp.bfloat16)
    hidden = lax.dot_general(
        normed_one, mlp_weight[0], contract_last, preferred_element_type=jnp.float32
    )
    active, gelu_back = jax.vjp(jax.nn.gelu, hidden)
    active_b = active.astype(jnp.bfloat16)
    branch_g = jnp.dot(active_b, mlp_weight[1], preferred_element_type=jnp.float32)
    input_two = (two_flat.astype(jnp.float32) - branch_g).astype(jnp.bfloat16)
    d_active = lax.dot_general(
        cot_two_flat, mlp_weight[1], contract_last, preferred_element_type=jnp.float32
    )
    d_down = lax.dot_general(
        active_b, cot_two_flat, contract_first, preferred_element_type=jnp.float32
    )
    d_hidden = gelu_back(d_active)[0].astype(jnp.bfloat16)
    d_up = lax.dot_general(d_hidden, normed_one, contract_first, preferred_element_type=jnp.float32)
    d_normed = jnp.dot(d_hidden, mlp_weight[0], preferred_element_type=jnp.float32)
    _, norm_back = jax.vjp(normalize, one_flat.astype(jnp.float32), norm_gain[0])
    d_first, d_gain_one = norm_back(d_normed)
    total_b = (cot_one_flat.astype(jnp.float32) + d_first).astype(jnp.bfloat16)
    normed_two = normalize(input_two.astype(jnp.float32), norm_gain[1]).astype(jnp.bfloat16)
    qkv_weight = jnp.concatenate([attn_weight[0], attn_weight[1], attn_weight[2]], axis=1)
    query = jnp.dot(normed_two, attn_weight[0], preferred_element_type=jnp.float32).astype(
        jnp.bfloat16
    )
    keyval = jnp.dot(normed_two, qkv_weight[:, width:], preferred_element_type=jnp.float32).astype(
        jnp.bfloat16
    )
    kv_frames = keyval.reshape(clips, frame_count, grid_rows, grid_cols, 2 * width)
    kv_padded = extended(kv_frames, (("tm", 1),), 1)
    kv_wide = kv_padded.astype(jnp.float32)
    pooled, pool_back = jax.vjp(partial(pool_frames, kv_wide), pool_kernel)
    pooled_b = pooled.astype(jnp.bfloat16)
    gathered = lax.all_gather(pooled_b, "tm", axis=1, tiled=True)
    key_count = gathered.shape[1]
    key_heads = gathered[:, :, :width].reshape(clips, key_count, heads, HEAD_DIM)
    value_heads = gathered[:, :, width:].reshape(clips, key_count, heads, HEAD_DIM)
    query_heads = query.reshape(clips, queries, heads, HEAD_DIM)
    scores = (
        jnp.einsum("cqhd,ckhd->chqk", query_heads, key_heads, preferred_element_type=jnp.float32)
        * score_scale
    )
    weights = jnp.exp(scores)
    probs = weights / jnp.sum(weights, axis=-1, keepdims=True)
    probs_b = probs.astype(jnp.bfloat16)
    attended = jnp.einsum(
        "chqk,ckhd->cqhd", probs_b, value_heads, preferred_element_type=jnp.float32
    )
    attended = attended.astype(jnp.bfloat16).reshape(rows, width)
    branch_f = jnp.dot(attended, attn_weight[3], preferred_element_type=jnp.float32)
    input_one = (one_flat.astype(jnp.float32) - branch_f).astype(jnp.bfloat16)
    d_out = lax.dot_general(attended, total_b, contract_first, preferred_element_type=jnp.float32)
    d_attended = lax.dot_general(
        total_b, attn_weight[3], contract_last, preferred_element_type=jnp.float32
    )
    d_attended = d_attended.astype(jnp.bfloat16).reshape(clips, queries, heads, HEAD_DIM)
    d_value = jnp.einsum("chqk,cqhd->ckhd", probs_b, d_attended, preferred_element_type=jnp.float32)
    d_probs = jnp.einsum(
        "cqhd,ckhd->chqk", d_attended, value_heads, preferred_element_type=jnp.float32
    )
    d_scores = (probs * (d_probs - jnp.sum(probs * d_probs, axis=-1, keepdims=True))).astype(
        jnp.bfloat16
    )
    d_query = (
        jnp.einsum("chqk,ckhd->cqhd", d_scores, key_heads, preferred_element_type=jnp.float32)
        * score_scale
    )
    d_query = d_query.astype(jnp.bfloat16).reshape(rows, width)
    d_key = (
        jnp.einsum("chqk,cqhd->ckhd", d_scores, query_heads, preferred_element_type=jnp.float32)
        * score_scale
    )
    d_pooled_all = jnp.concatenate(
        [d_key.reshape(clips, key_count, width), d_value.reshape(clips, key_count, width)], axis=-1
    )
    d_pooled = lax.psum_scatter(
        d_pooled_all.astype(jnp.bfloat16), "tm", scatter_dimension=1, tiled=True
    ).astype(jnp.float32)
    d_kernel = pool_back(d_pooled)[0]
    d_rims = extended(
        d_pooled.reshape(clips, frame_count, 16, 2 * width).astype(jnp.bfloat16), (("tm", 1),), 1
    ).astype(jnp.float32)
    _, frame_back = jax.vjp(
        partial(pool_widened, kernel=pool_kernel), kv_frames.astype(jnp.float32)
    )
    d_keyval = frame_back(d_rims.reshape(clips, (frame_count + 2) * 16, 2 * width))[0]
    d_keyval = d_keyval.reshape(rows, 2 * width).astype(jnp.bfloat16)
    d_proj = jnp.concatenate([d_query, d_keyval], axis=1)
    d_normed_two = lax.dot_general(
        d_proj, qkv_weight, contract_last, preferred_element_type=jnp.float32
    )
    d_qkv = lax.dot_general(normed_two, d_proj, contract_first, preferred_element_type=jnp.float32)
    _, norm_back_two = jax.vjp(normalize, input_two.astype(jnp.float32), norm_gain[1])
    d_second, d_gain_two = norm_back_two(d_normed_two)
    input_grad_two = (cot_two_flat.astype(jnp.float32) + d_second).astype(jnp.bfloat16)
    attn_part = jnp.stack(
        [d_qkv[:, :width], d_qkv[:, width : 2 * width], d_qkv[:, 2 * width :], d_out]
    )
    mlp_part = jnp.stack([d_up, d_down])
    gain_part = jnp.stack([d_gain_one, d_gain_two])
    summed = (
        lax.psum_scatter(attn_part, ("clip", "tm"), scatter_dimension=2, tiled=True),
        lax.psum_scatter(mlp_part, ("clip", "tm"), scatter_dimension=2, tiled=True),
        lax.psum_scatter(d_kernel, ("clip", "tm"), scatter_dimension=3, tiled=True),
        lax.psum_scatter(gain_part, ("clip", "tm"), scatter_dimension=1, tiled=True),
    )
    shape_out = half_one.shape
    return (
        input_one.reshape(shape_out),
        input_two.reshape(shape_out),
        total_b.reshape(shape_out),
        input_grad_two.reshape(shape_out),
        summed[0],
        summed[1],
        summed[2],
        summed[3],
    )


def solution(mesh):
    placed = (
        P("clip", "tm", None, None, None),
        P("clip", "tm", None, None, None),
        P("clip", "tm", None, None, None),
        P("clip", "tm", None, None, None),
        P(),
        P(),
        P(),
        P(),
    )
    return jax.shard_map(
        shards,
        mesh=mesh,
        in_specs=placed,
        out_specs=(
            P("clip", "tm", None, None, None),
            P("clip", "tm", None, None, None),
            P("clip", "tm", None, None, None),
            P("clip", "tm", None, None, None),
            P(None, None, ("clip", "tm")),
            P(None, None, ("clip", "tm")),
            P(None, None, None, ("clip", "tm")),
            P(None, ("clip", "tm")),
        ),
        check_vma=False,
    )
```

profile of v0, /device:TPU:1, one launch (start us, length us, event | category | flops | bytes accessed | tf_op | source)
XLA Modules:
  0.0 697.1 jit_solution(1462848527563303513)
XLA Ops:
  12.7 4.1 fusion.6
  16.9 4.9 convert_reduce_fusion
  27.0 4.7 collective-permute-start
  31.8 12.7 %collective-permute-done.1 = bf16[1,1,14,14,1536]{4,3,2,1,0:T(8,128)(2,1)S(1)} collective-permute-done((bf16[1,1,14,14,1536]{4,3,2,1,0:T(8,128)(2,1)S(1)}, bf16[1,1,14,14,1536]{4,3,2,1,0:T(8,128)(2,1)S(1)}, u32[]{:S(2)}, u32[]{:S(2)}) %collective-permute-start.1) | collective-permute-done | bytes 602144 | tf_op jit(solution)/shard_map/ppermute | solution.py:19
  44.5 15.6 %collective-permute-done = bf16[1,1,14,14,1536]{4,3,2,1,0:T(8,128)(2,1)S(1)} collective-permute-done((bf16[1,1,14,14,1536]{4,3,2,1,0:T(8,128)(2,1)S(1)}, bf16[1,1,14,14,1536]{4,3,2,1,0:T(8,128)(2,1)S(1)}, u32[]{:S(2)}, u32[]{:S(2)}) %collective-permute-start) | collective-permute-done | bytes 602144 | tf_op jit(solution)/shard_map/ppermute | solution.py:16
  60.1 2.1 select_maximum_fusion
  62.2 4.0 reshape.389
  70.3 1.9 reshape.400
  72.2 1.9 reshape.412
  76.0 5.6 fusion.29
  81.7 4.7 multiply_reduce_fusion.8
  86.9 1.9 convolution_convert_fusion.3
  89.7 113.6 %all-gather.2.cloned.1.call-done = bf16[1,512,1536]{2,1,0:T(8,128)(2,1)} async-done(((bf16[1,16,1536]{2,1,0:T(8,128)(2,1)}), bf16[1,512,1536]{2,1,0:T(8,128)(2,1)}) %all-gather.2.cloned.1.call-update) | async-done | bytes 1572880 | tf_op jit(solution)/shard_map/all_gather | solution.py:93
  209.9 3.7 multiply_reduce_fusion
  216.5 2.3 copy.40
  218.8 2.6 pad_maximum_fusion.2
  221.7 3.2 convolution_bitcast_fusion.1
  224.9 2.0 convolution_bitcast_fusion
  226.9 6.9 pad_maximum_fusion
  233.8 28.4 %copy.44 = f32[2,3072,768]{1,0,2:T(2,128)} copy(f32[2,3072,768]{2,1,0:T(8,128)} %pad_maximum_fusion) | data formatting | bytes 37748736 | tf_op jit(solution)/shard_map/stack | solution.py:158
  262.1 2.0 fusion.38
  265.1 3.8 convolution_convert_fusion.2
  271.5 109.1 %reduce-scatter.4.cloned.1.call-done = bf16[1,16,1536]{2,1,0:T(8,128)(2,1)} async-done(((bf16[1,512,1536]{2,1,0:T(8,128)(2,1)}), bf16[1,16,1536]{2,1,0:T(8,128)(2,1)}) %reduce-scatter.4.cloned.1.call-update) | async-done | bytes 49168 | tf_op jit(solution)/shard_map/reduce_scatter | solution.py:135
  381.8 4.2 collective-permute-start.2
  389.8 4.6 multiply_bitcast_fusion.2
  394.4 3.5 add_convert_fusion
  397.9 7.2 %reshape.405 = bf16[1,5,16,16,1536]{4,3,2,1,0:T(8,128)(2,1)} reshape(bf16[1,5,4,4,4,4,1536]{6,5,4,3,2,1,0:T(4,128)(2,1)} %add_convert_fusion) | data formatting | bytes 7864320 | tf_op jit(solution)/shard_map/transpose(jvp())/reshape | solution.py:34
  409.6 4.0 pad_maximum_fusion.1
  413.6 12.0 %copy.43 = f32[4,768,768]{1,0,2:T(4,128)} copy(f32[4,768,768]{2,1,0:T(8,128)} %pad_maximum_fusion.1) | data formatting | bytes 18874368 | tf_op jit(solution)/shard_map/stack | solution.py:155
  430.1 3.2 fusion.61
  434.8 89.2 %all-reduce.11 = f32[2,768]{1,0:T(2,128)S(1)} all-reduce(f32[2,768]{1,0:T(2,128)S(1)} %pad_maximum_fusion.6), channel_id=6, replica_groups=mesh['clip'=4,'tm'=32] {'clip','tm'}, use_global_device_ids=true, to_apply=%region_16.17.clone | all-reduce | flops 1536 | bytes 12288
  524.7 161.3 %all-reduce.15.cloned.1.call-done = (f32[4,768,768]{1,0,2:T(4,128)}, f32[2,3072,768]{1,0,2:T(2,128)}, f32[3,4,4,1536]{3,2,1,0:T(4,128)}) async-done(((f32[4,768,768]{1,0,2:T(4,128)}, f32[2,3072,768]{1,0,2:T(2,128)}, f32[3,4,4,1536]{3,2,1,0:T(4,128)}), (f32[4,768,768]{1,0,2:T(4,128)}, f32[2,3072,768]{1,0,2:T(2,128)}, f32[3,4,4,1536]{3,2,1,0:T(4,128)})) %all-reduce.15.cloned.1.call-update) | async-done | bytes 28606480
  (156 shorter events, 51.7 us)
Async XLA Ops:
  7.2 196.1 %all-gather.2.cloned.1.call-start = ((), (), s32[]{:S(2)}) async-start(), calls=%async_computation.1 | async-start | bytes 1622016 | tf_op jit(solution)/shard_map/all_gather | solution.py:93
  12.7 9.3 %slice-start.2 = ((s8[4718592]{0:T(1024)(128)(4,1)}), s8[4194304]{0:T(1024)(128)(4,1)S(1)}, s32[]{:S(2)}) async-start(s8[4718592]{0:T(1024)(128)(4,1)} %bitcast.177), calls=%async_computation.6 | async-start | bytes 8388608
  16.8 4.9 copy-start.7
  16.9 5.2 slice-start.3
  21.8 52.3 %copy-start.28 = (f32[196]{0:T(256)}, f32[196]{0:T(256)S(1)}, u32[]{:S(2)}) copy-start(f32[196]{0:T(256)S(1)} %broadcast_multiply_fusion.1) | copy-start | bytes 2356
  22.1 52.0 %copy-start.30 = (f32[196]{0:T(256)}, f32[196]{0:T(256)S(1)}, u32[]{:S(2)}) copy-start(f32[196]{0:T(256)S(1)} %fusion.67) | copy-start | bytes 2356
  24.8 6.9 copy-start.27
  25.7 18.8 %collective-permute-start.1 = (bf16[1,1,14,14,1536]{4,3,2,1,0:T(8,128)(2,1)S(1)}, bf16[1,1,14,14,1536]{4,3,2,1,0:T(8,128)(2,1)S(1)}, u32[]{:S(2)}, u32[]{:S(2)}) collective-permute-start(bf16[1,1,14,14,1536]{4,3,2,1,0:T(8,128)(2,1)S(1)} %reshape.388), channel_id=1, source_target_pairs={{1,0},{2,1},{3,2},{4,3},{5,4},{6,5},{7,6},{8,7},{9,8},{10,9},{11,1... | collective-permute-start | bytes 1806344 | tf_op jit(solution)/shard_map/ppermute | solution.py:19
  27.0 33.1 %collective-permute-start = (bf16[1,1,14,14,1536]{4,3,2,1,0:T(8,128)(2,1)S(1)}, bf16[1,1,14,14,1536]{4,3,2,1,0:T(8,128)(2,1)S(1)}, u32[]{:S(2)}, u32[]{:S(2)}) collective-permute-start(bf16[1,1,14,14,1536]{4,3,2,1,0:T(8,128)(2,1)S(1)} %reshape.388), channel_id=1, source_target_pairs={{0,1},{1,2},{2,3},{3,4},{4,5},{5,6},{6,7},{7,8},{8,9},{9,10},{10,1... | collective-permute-start | bytes 1806344 | tf_op jit(solution)/shard_map/ppermute | solution.py:16
  31.8 34.5 %copy-start.23 = (f32[1536,4,4]{0,2,1:T(4,128)}, f32[1536,4,4]{0,2,1:T(4,128)S(1)}, u32[]{:S(2)}) copy-start(f32[1536,4,4]{0,2,1:T(4,128)S(1)} %get-tuple-element.54) | copy-start | bytes 294916
  66.3 5.9 copy-start
  68.8 311.8 %reduce-scatter.4.cloned.1.call-start = ((), (), s32[]{:S(2)}) async-start(), calls=%async_computation.2 | async-start | bytes 1622016 | tf_op jit(solution)/shard_map/reduce_scatter | solution.py:135
  70.2 16.2 %copy-start.5 = (f32[196,768]{1,0:T(8,128)}, f32[196,768]{1,0:T(8,128)S(1)}, u32[]{:S(2)}) copy-start(f32[196,768]{1,0:T(8,128)S(1)} %reshape.410) | copy-start | bytes 1806340
  74.1 2.0 copy-start.14
  76.0 129.3 %copy-start.9 = (bf16[196,768]{0,1:T(8,128)(2,1)}, bf16[196,768]{0,1:T(8,128)(2,1)S(1)}, u32[]{:S(2)}) copy-start(bf16[196,768]{0,1:T(8,128)(2,1)S(1)} %copy.37) | copy-start | bytes 903172
  81.7 4.7 copy-start.18
  81.7 5.0 copy-start.17
  86.9 2.9 copy-start.11
  205.4 4.5 copy-start.24
  206.5 2.2 copy-start.2
  209.9 3.7 slice-start
  209.9 3.8 slice-start.1
  221.4 3.5 copy-start.15
  221.4 464.6 %all-reduce.15.cloned.1.call-start = ((), (), s32[]{:S(2)}) async-start(), calls=%async_computation.3 | async-start | bytes 57212928
  221.7 3.2 copy-start.8
  265.1 4.6 copy-start.12
  268.9 118.1 %copy-start.1 = (bf16[1,3,4,4,4,4,1536]{6,5,4,3,2,1,0:T(4,128)(2,1)S(1)}, bf16[1,3,4,4,4,4,1536]{6,5,4,3,2,1,0:T(4,128)(2,1)}, u32[]{:S(2)}) copy-start(bf16[1,3,4,4,4,4,1536]{6,5,4,3,2,1,0:T(4,128)(2,1)} %copy-done) | copy-start | bytes 7077892
  380.5 8.4 %collective-permute-start.3 = (bf16[1,1,16,1536]{3,2,1,0:T(8,128)(2,1)}, bf16[1,1,16,1536]{3,2,1,0:T(8,128)(2,1)S(1)}, u32[]{:S(2)}, u32[]{:S(2)}) collective-permute-start(bf16[1,1,16,1536]{3,2,1,0:T(8,128)(2,1)} %bitcast.190), channel_id=1, source_target_pairs={{1,0},{2,1},{3,2},{4,3},{5,4},{6,5},{7,6},{8,7},{9,8},{10,9},{11,1... | collective-permute-start | bytes 147464 | tf_op jit(solution)/shard_map/ppermute | solution.py:19
  381.8 7.1 %collective-permute-start.2 = (bf16[1,1,16,1536]{3,2,1,0:T(8,128)(2,1)}, bf16[1,1,16,1536]{3,2,1,0:T(8,128)(2,1)S(1)}, u32[]{:S(2)}, u32[]{:S(2)}) collective-permute-start(bf16[1,1,16,1536]{3,2,1,0:T(8,128)(2,1)} %bitcast.191), channel_id=1, source_target_pairs={{0,1},{1,2},{2,3},{3,4},{4,5},{5,6},{6,7},{7,8},{8,9},{9,10},{10,1... | collective-permute-start | bytes 147464 | tf_op jit(solution)/shard_map/ppermute | solution.py:16
  425.7 4.4 copy-start.20
  430.1 3.2 copy-start.33
  430.1 3.6 copy-start.16
  (14 other events, 19.3 us)
Sparse Core Ops, SparseCore 0:
  68.9 134.3 all-gather.1
  221.5 158.9 reduce-scatter.3
  425.8 260.1 all-reduce.14
where the time goes:
time: 699 us; the launch traced here: 697 us
  waiting for transfers between devices  412 us (59%)
  blocking collectives  89.2 us (13%)
  local copies, waits for them, and re-layouts  84 us (12%)
  matrix products  50.5 us (7%)
  other arithmetic  34.5 us (5%)
  between operations  14.5 us (2%)
  starting transfers between devices  12 us (2%)
    unnamed x4, waiting for transfers between devices  161 us
    all_gather x1, waiting for transfers between devices, shards(): gathered = lax.all_gather(pooled_b, 'tm', axis=1, tiled=True)  114 us
    reduce_scatter x1, waiting for transfers between devices, shards(): lax.psum_scatter(d_pooled_all.astype(jnp.bfloat16), 'tm', scatter_dimensi...  109 us
    unnamed x1, blocking collectives  89.2 us
    another operation x1, local copies, waits for them, and re-layouts, shards(): mlp_part = jnp.stack([d_up, d_down])  28.4 us
    ppermute x2, waiting for transfers between devices, extended(): lax.ppermute(lax.slice_in_dim(block, block.shape[dim] - width, None, axis...  15.6 us
  transfers between devices with their start and end apart: 7, of which 5 were waited for; matrix products, arithmetic and copies ran while one was open for 12% of the time, Pallas kernels for 0%

commit v1 on v0

v1 whole, which is shorter than its diff:
```python
from functools import partial

import jax
import jax.numpy as jnp
from jax import lax
from jax.experimental import pallas as pl
from jax.experimental.pallas import tpu as pltpu
from jax.sharding import PartitionSpec as P

D = 768
FF = 3072
KV = 2 * D
ROWS = 224
CHUNK = 512
STEPS = FF // CHUNK
HALF = 384
MIB = 1024 * 1024
F32 = jnp.float32
BF16 = jnp.bfloat16
MESH = pl.DeviceIdType.MESH


def dot(a, b):
    return lax.dot_general(a, b, (((1,), (0,)), ((), ())), preferred_element_type=F32)


def dot_nt(a, b):
    return lax.dot_general(a, b, (((1,), (1,)), ((), ())), preferred_element_type=F32)


def dot_tn(a, b):
    return lax.dot_general(a, b, (((0,), (0,)), ((), ())), preferred_element_type=F32)


def iota(shape, dim):
    return lax.broadcasted_iota(jnp.int32, shape, dim)


def source_column(rows, part):
    owner_at = (rows * 43691) >> 18
    inner = rows - owner_at * 6
    core = owner_at >> 6
    digits = ((owner_at >> 4) & 3, (owner_at >> 2) & 3, owner_at & 3)
    x, y, z = (digits[(axis - part) % 3] for axis in range(3))
    owner = (y >> 1) * 64 + core * 32 + x * 8 + z * 2 + (y & 1)
    return owner * 6 + inner


def permutation(part):
    source = source_column(iota((D, 128), 0), part)
    lanes = iota((D, 128), 1)
    pieces = [
        jnp.where(source == lanes + 128 * k, 1.0, 0.0).astype(BF16) for k in range(D // 128)
    ]
    return jnp.concatenate(pieces, axis=1)


def norm_stats(values):
    centre = jnp.mean(values, axis=-1, keepdims=True)
    centred = values - centre
    spread = jnp.mean(centred * centred, axis=-1, keepdims=True)
    scale = lax.rsqrt(spread + 1e-05)
    return centred * scale, scale


def norm_back(unit, scale, gain, cotangent):
    d_unit = cotangent * gain
    first = jnp.mean(d_unit, axis=-1, keepdims=True)
    second = jnp.mean(d_unit * unit, axis=-1, keepdims=True)
    return scale * (d_unit - first - unit * second)


def load_padded(ref, pad):
    pad[...] = jnp.zeros(pad.shape, pad.dtype)
    pad[:, 0:14, :] = ref[0, 0]
    return pad[...].reshape(ROWS, D)


def store_grid(ref, values):
    ref[0, 0] = values.reshape(14, 16, D)[:, 0:14, :]


def cell_maps():
    row = iota((ROWS, 48), 0)
    across, down = (row & 15) + 1, (row >> 4) + 1
    valid = across < 15
    cell = (down & 3) * 4 + (across & 3)
    lane = iota((ROWS, 48), 1)
    cells = jnp.where(valid & ((lane & 15) == cell), 1.0, 0.0).astype(BF16)
    row = iota((ROWS, 16), 0)
    across, down = (row & 15) + 1, (row >> 4) + 1
    block = (down >> 2) * 4 + (across >> 2)
    blocks = jnp.where((across < 15) & (iota((ROWS, 16), 1) == block), 1.0, 0.0).astype(BF16)
    return cells, blocks


def spread_kernel(cells, flat):
    high = flat.astype(BF16)
    rest = flat - high.astype(F32)
    middle = rest.astype(BF16)
    low = (rest - middle.astype(F32)).astype(BF16)
    return dot(cells, jnp.concatenate([high, middle, low], axis=0))


def gather_rows(one_hot, values):
    high = values.astype(BF16)
    low = (values - high.astype(F32)).astype(BF16)
    return dot_tn(one_hot, high) + dot_tn(one_hot, low)


def mlp_kernel(
    one_ref, two_ref, cot_one_ref, cot_two_ref, gain_ref, up_ref, down_ref, attn_hbm, pool_ref,
    two_out, total_out, grad_out, normed_out, query_out, keyval_out, datt_out, total_pad_out,
    part_out, gain_out,
    pad, normed, cot, left, branch, d_normed, attn, pool, sem,
):
    step = pl.program_id(0)
    attn_copy = pltpu.make_async_copy(attn_hbm, attn, sem)

    @pl.when(step == 0)
    def _():
        attn_copy.start()
        unit, _ = norm_stats(load_padded(one_ref, pad).astype(F32))
        normed[...] = (unit * gain_ref[0:1, :]).astype(BF16)
        cot[...] = load_padded(cot_two_ref, pad)
        branch[...] = jnp.zeros(branch.shape, F32)
        d_normed[...] = jnp.zeros(d_normed.shape, F32)

    @pl.when(step % 2 == 0)
    def _():
        for part in range(3):

            @pl.when(step == 2 * part)
            def _():
                order = permutation(part)
                left[0] = dot_nt(order, normed[...]).astype(BF16)
                left[1] = dot_nt(order, cot[...]).astype(BF16)

    hidden = dot_nt(normed[...], up_ref[0])
    inner = 0.7978845608028654 * (hidden + 0.044715 * hidden * hidden * hidden)
    tanh = jnp.tanh(inner)
    half_sum = 0.5 * (1.0 + tanh)
    active = (hidden * half_sum).astype(BF16)
    slope = half_sum + 0.5 * hidden * (1.0 - tanh * tanh) * (
        0.7978845608028654 * (1.0 + 3.0 * 0.044715 * hidden * hidden)
    )
    d_hidden = (slope * dot_nt(cot[...], down_ref[0])).astype(BF16)
    branch[...] += dot(active, down_ref[0])
    d_normed[...] += dot(d_hidden, up_ref[0])
    grad_out[:, 0:CHUNK] = dot(left[0], d_hidden).astype(BF16)
    grad_out[:, CHUNK:] = dot(left[1], active).astype(BF16)

    @pl.when(step == STEPS - 1)
    def _():
        attn_copy.wait()
        unit, scale = norm_stats(load_padded(one_ref, pad).astype(F32))
        back = d_normed[...]
        gain_out[...] = jnp.sum(back * unit, axis=0, keepdims=True)
        d_first = norm_back(unit, scale, gain_ref[0:1, :], back)
        total = (load_padded(cot_one_ref, pad).astype(F32) + d_first).astype(BF16)
        store_grid(total_out, total)
        total_pad_out[...] = total
        datt_out[...] = dot_nt(total, attn[3]).astype(BF16)
        restored = (load_padded(two_ref, pad).astype(F32) - branch[...]).astype(BF16)
        store_grid(two_out, restored)
        unit_two, _ = norm_stats(restored.astype(F32))
        normed_two = (unit_two * gain_ref[1:2, :]).astype(BF16)
        normed_out[...] = normed_two
        query_out[...] = dot(normed_two, attn[0]).astype(BF16)
        keyval_out[:, 0:D] = dot(normed_two, attn[1]).astype(BF16)
        keyval_out[:, D:] = dot(normed_two, attn[2]).astype(BF16)
        cells, blocks = cell_maps()
        for offset in range(3):
            for i in range(4):
                pool[4 * i : 4 * i + 4, :] = pool_ref[offset, i]
            weighted = spread_kernel(cells, pool[...]) * keyval_out[...].astype(F32)
            part_out[offset] = gather_rows(blocks, weighted)


def run_mlp(half_one, half_two, grad_one, grad_two, norm_gain, attn_weight, mlp_weight, pool_kernel):
    grid_block = pl.BlockSpec((1, 1, 14, 14, D), lambda f: (0, 0, 0, 0, 0))

    def whole(*shape):
        return pl.BlockSpec(shape, lambda f: (0,) * len(shape))

    shape = jax.ShapeDtypeStruct
    return pl.pallas_call(
        mlp_kernel,
        grid=(STEPS,),
        in_specs=[
            grid_block, grid_block, grid_block, grid_block,
            whole(2, D),
            pl.BlockSpec((1, CHUNK, D), lambda f: (0, f, 0)),
            pl.BlockSpec((1, CHUNK, D), lambda f: (1, f, 0)),
            pl.BlockSpec(memory_space=pl.ANY),
            whole(3, 4, 4, KV),
        ],
        out_specs=[
            grid_block, grid_block,
            pl.BlockSpec((D, 2 * CHUNK), lambda f: (0, f)),
            whole(ROWS, D), whole(ROWS, D), whole(ROWS, KV), whole(ROWS, D), whole(ROWS, D),
            whole(3, 16, KV), whole(1, D),
        ],
        out_shape=[
            shape(half_one.shape, BF16), shape(half_one.shape, BF16),
            shape((D, 2 * FF), BF16),
            shape((ROWS, D), BF16), shape((ROWS, D), BF16), shape((ROWS, KV), BF16),
            shape((ROWS, D), BF16), shape((ROWS, D), BF16),
            shape((3, 16, KV), F32), shape((1, D), F32),
        ],
        scratch_shapes=[
            pltpu.VMEM((14, 16, D), BF16),
            pltpu.VMEM((ROWS, D), BF16),
            pltpu.VMEM((ROWS, D), BF16),
            pltpu.VMEM((2, D, ROWS), BF16),
            pltpu.VMEM((ROWS, D), F32),
            pltpu.VMEM((ROWS, D), F32),
            pltpu.VMEM((4, D, D), BF16),
            pltpu.VMEM((16, KV), F32),
            pltpu.SemaphoreType.DMA,
        ],
        compiler_params=pltpu.CompilerParams(
            dimension_semantics=("arbitrary",), vmem_limit_bytes=48 * MIB
        ),
        name="mlp_branch",
    )(half_one, half_two, grad_one, grad_two, norm_gain, mlp_weight, mlp_weight, attn_weight, pool_kernel)


class Links:
    def __init__(self, send, recv):
        self.send, self.recv, self.used, self.started = send, recv, 0, []

    def start(self, source, target, device):
        copy = pltpu.make_async_remote_copy(
            src_ref=source, dst_ref=target,
            send_sem=self.send.at[self.used], recv_sem=self.recv.at[self.used],
            device_id=device, device_id_type=MESH,
        )
        self.used += 1
        copy.start()
        self.started.append(copy)
        return copy


class Place:
    def __init__(self):
        clip, tm = lax.axis_index("clip"), lax.axis_index("tm")
        self.tm, self.clip = tm, clip
        self.core, high = clip % 2, clip // 2
        self.low = tm % 2
        self.at = (tm // 8, high * 2 + self.low, (tm // 2) % 4)

    def device(self, core, at):
        x, y, z = at
        return ((y // 2) * 2 + core, x * 8 + z * 2 + y % 2)

    def other_core(self):
        return self.device(1 - self.core, self.at)

    def along(self, axis, hop):
        at = list(self.at)
        at[axis] = (at[axis] + hop) % 4
        return self.device(self.core, at), at[axis]

    def pair(self):
        return (self.clip, self.tm - self.low + (1 - self.low))

    def frame(self, hop):
        return (self.clip, (self.tm + hop + 32) % 32)


class Reduction:
    def __init__(self, links, place, parts, full, held, base, landed, out, out_base):
        self.links, self.place, self.parts = links, place, parts
        self.full, self.held, self.base = full, held, base
        self.in0, self.in1, self.sum1, self.in2, self.sum2, self.in3 = landed
        self.out, self.out_base = out, out_base
        self.copies = {}

    def columns(self, part):
        return pl.ds(self.parts[part][0], self.parts[part][1])

    def blocks(self, part, width=512):
        first, count = self.parts[part]
        if count % width:
            width = count
        return [(first + k * width, width) for k in range(count // width)]

    def send0(self, part):
        cols = self.columns(part)
        rows = pl.ds(pl.multiple_of((1 - self.place.core) * HALF, HALF), HALF)
        self.copies[0, part] = [
            self.links.start(
                self.full.at[rows, cols], self.in0.at[:, cols], self.place.other_core()
            )
        ]

    def arrive(self, stage, part):
        for copy in self.copies[stage, part]:
            copy.wait_recv()

    def spread(self, stage, part, source, base, rows, target):
        axis = (part + stage - 1) % 3
        cols = self.columns(part)
        self.copies[stage, part] = []
        for hop in (2, 1, 3):
            device, at = self.place.along(axis, hop)
            window = pl.ds(pl.multiple_of(base + at * rows, rows), rows)
            self.copies[stage, part].append(
                self.links.start(source.at[window, cols], target.at[hop - 1, :, cols], device)
            )

    def send1(self, part):
        self.arrive(0, part)
        first, count = self.parts[part]

        def body(k, carry):
            rows = pl.ds(pl.multiple_of(k * 16, 16), 16)
            mine = pl.ds(pl.multiple_of(self.base + k * 16, 16), 16)
            cols = pl.ds(first, count)
            total = self.held[mine, cols].astype(F32) + self.in0[rows, cols].astype(F32)
            self.held[mine, cols] = total.astype(BF16)
            return carry

        lax.fori_loop(0, HALF // 16, body, 0)
        self.spread(1, part, self.held, self.base, 96, self.in1)

    def send2(self, part):
        self.arrive(1, part)
        mine = self.place.at[part % 3]
        rows = pl.ds(pl.multiple_of(self.base + mine * 96, 96), 96)
        place_row, place_col = iota((128, 96), 0), iota((128, 96), 1)
        owner = place_row >> 3
        inner = place_row & 7
        widen = jnp.where((inner < 6) & (place_col == owner * 6 + inner), 1.0, 0.0).astype(BF16)
        for first, count in self.blocks(part):
            cols = pl.ds(first, count)
            total = self.held[rows, cols].astype(F32)
            for slot in range(3):
                total = total + self.in1[slot, :, cols].astype(F32)
            self.sum1[:, cols] = dot(widen, total.astype(BF16)).astype(BF16)
        self.spread(2, part, self.sum1, 0, 32, self.in2)

    def send3(self, part):
        self.arrive(2, part)
        mine = self.place.at[(part + 1) % 3]
        rows = pl.ds(pl.multiple_of(mine * 32, 32), 32)
        for first, count in self.blocks(part):
            cols = pl.ds(first, count)
            total = self.sum1[rows, cols].astype(F32)
            for slot in range(3):
                total = total + self.in2[slot, :, cols].astype(F32)
            self.sum2[:, cols] = total
        self.spread(3, part, self.sum2, 0, 8, self.in3)

    def finish(self, part):
        self.arrive(3, part)
        mine = self.place.at[(part + 2) % 3]
        rows = pl.ds(pl.multiple_of(mine * 8, 8), 8)
        for first, count in self.blocks(part):
            cols = pl.ds(first, count)
            total = self.sum2[rows, cols]
            for slot in range(3):
                total = total + self.in3[slot, :, cols]
            self.out[:, pl.ds(self.out_base + first, count)] = total


MLP_PARTS = tuple((p * 2048, 2048) for p in range(3))
FIRST_PARTS = tuple((p * 512, 512) for p in range(3))
LAST_PARTS = ((0, 512), (512, 512), (1024, 640))
MLP_COLS, FIRST_COLS, LAST_COLS = 6144, 1536, 1664
N_COPIES = 3 * 30 + 2 * 14 + 4


def landing(cols):
    return [
        pltpu.VMEM((HALF, cols), BF16),
        pltpu.VMEM((3, 96, cols), BF16),
        pltpu.VMEM((128, cols), BF16),
        pltpu.VMEM((3, 32, cols), BF16),
        pltpu.VMEM((32, cols), F32),
        pltpu.VMEM((3, 8, cols), F32),
    ]


def attention_kernel(
    query_ref, keyval_ref, datt_ref, total_ref, normed_ref, parts_ref, gain_one_ref,
    one_ref, two_ref, cot_two_ref, gain_ref, pool_ref, attn_hbm, mlp_hbm,
    one_out, grad_two_out, sums_out,
    *scratch,
):
    scratch = list(scratch)

    def take(count):
        taken = scratch[:count]
        del scratch[:count]
        return taken

    send_sem, recv_sem, local_sem = take(3)
    mlp_own, mlp_land = take(1)[0], take(6)
    first_full, first_land = take(1)[0], take(6)
    last_full, last_land = take(1)[0], take(6)
    attn, spread, orders, pool, halo, pooled, pad = take(7)
    keys, values, d_keys, d_values = take(4)
    x_keys, z_keys, y_keys, x_values, z_values, y_values = take(6)
    key_sum, value_sum, key_pair, value_pair = take(4)
    d_pooled, d_halo = take(2)
    attended, d_query, extra, extra_gain = take(4)

    place = Place()
    links = Links(send_sem, recv_sem)
    x, y, z = place.at
    low = place.low

    barrier = pltpu.get_barrier_semaphore()
    partners = [place.other_core(), place.frame(1), place.frame(-1)]
    partners += [place.along(axis, hop)[0] for axis in range(3) for hop in (1, 2, 3)]
    for device in partners:
        pl.semaphore_signal(barrier, inc=1, device_id=device, device_id_type=MESH)
    pl.semaphore_wait(barrier, len(partners))

    halo_copies = [
        links.start(parts_ref.at[0], halo.at[0], place.frame(1)),
        links.start(parts_ref.at[2], halo.at[1], place.frame(-1)),
    ]
    mlp = Reduction(links, place, MLP_PARTS, mlp_hbm, mlp_own, 0, mlp_land, sums_out, 0)
    first = Reduction(
        links, place, FIRST_PARTS, first_full, first_full, place.core * HALF, first_land,
        sums_out, MLP_COLS,
    )
    last = Reduction(
        links, place, LAST_PARTS, last_full, last_full, place.core * HALF, last_land,
        sums_out, MLP_COLS + FIRST_COLS,
    )
    own_rows = pl.ds(pl.multiple_of(place.core * HALF, HALF), HALF)
    own_copies = []
    for part in range(3):
        mlp.send0(part)
        cols = mlp.columns(part)
        own_copies.append(
            pltpu.make_async_copy(
                mlp_hbm.at[own_rows, cols], mlp_own.at[:, cols], local_sem.at[part]
            )
        )
        own_copies[-1].start()
    attn_copy = pltpu.make_async_copy(attn_hbm, attn, local_sem.at[3])
    attn_copy.start()

    for copy in halo_copies:
        copy.wait_recv()
    from_left = jnp.where(place.tm > 0, halo[0], 0.0)
    from_right = jnp.where(place.tm < 31, halo[1], 0.0)
    pooled[...] = (parts_ref[1] + from_left + from_right).astype(BF16)
    at_low = pl.ds(pl.multiple_of(low * 16, 16), 16)
    keys[x, z, at_low, :] = pooled[:, 0:D]
    values[x, z, at_low, :] = pooled[:, D:]

    copies = [
        links.start(keys.at[x, z, at_low, :], keys.at[x, z, at_low, :], place.pair()),
        links.start(values.at[x, z, at_low, :], values.at[x, z, at_low, :], place.pair()),
    ]
    cells, blocks = cell_maps()
    for offset in range(3):
        for i in range(4):
            pool[4 * i : 4 * i + 4, :] = pool_ref[offset, i]
        spread[offset] = spread_kernel(cells, pool[...])
    for copy in copies:
        copy.wait_recv()
    copies = []
    for hop in (2, 1, 3):
        copies.append(links.start(keys.at[x, z], keys.at[x, z], place.along(2, hop)[0]))
        copies.append(links.start(values.at[x, z], values.at[x, z], place.along(0, hop)[0]))
    for part in range(3):
        orders[part] = permutation(part)
    for copy in copies:
        copy.wait_recv()
    copies = []
    for hop in (2, 1, 3):
        copies.append(links.start(keys.at[x], keys.at[x], place.along(0, hop)[0]))
        copies.append(links.start(values.at[:, z], values.at[:, z], place.along(2, hop)[0]))
    for copy in own_copies:
        copy.wait()
    for copy in copies:
        copy.wait_recv()
    for part in range(3):
        mlp.send1(part)

    def heads(pair, carry):
        lanes = pl.ds(pl.multiple_of(pair * 128, 128), 128)
        query = query_ref[:, lanes]
        d_att = datt_ref[:, lanes]
        key = keys[:, :, :, lanes].reshape(512, 128)
        value = values[:, :, :, lanes].reshape(512, 128)
        att = d_q = d_k = d_v = None
        for side in range(2):

            def only(array):
                lane = iota(array.shape, 1)
                keep = lane < 64 if side == 0 else lane >= 64
                return jnp.where(keep, array, jnp.zeros_like(array))

            query_h, d_att_h = only(query), only(d_att)
            weights = jnp.exp(dot_nt(query_h, key) * 0.125)
            probs = weights * (1.0 / jnp.sum(weights, axis=-1, keepdims=True))
            probs_b = probs.astype(BF16)
            d_probs = dot_nt(d_att_h, value)
            product = probs * d_probs
            d_scores = (product - probs * jnp.sum(product, axis=-1, keepdims=True)).astype(BF16)
            terms = (
                dot(probs_b, only(value)), dot(d_scores, only(key)),
                dot_tn(d_scores, query_h), dot_tn(probs_b, d_att_h),
            )
            if side == 0:
                att, d_q, d_k, d_v = terms
            else:
                att, d_q, d_k, d_v = (a + b for a, b in zip((att, d_q, d_k, d_v), terms))
        attended[:, lanes] = att.astype(BF16)
        d_query[:, lanes] = (d_q * 0.125).astype(BF16)
        d_keys[:, :, :, lanes] = (d_k * 0.125).astype(BF16).reshape(4, 4, 32, 128)
        d_values[:, :, :, lanes] = d_v.astype(BF16).reshape(4, 4, 32, 128)
        return carry

    lax.fori_loop(0, 6, heads, 0)

    copies = []
    for hop in (2, 1, 3):
        device, at = place.along(0, hop)
        copies.append(links.start(d_keys.at[at], x_keys.at[hop - 1], device))
        device, at = place.along(2, hop)
        copies.append(links.start(d_values.at[:, at], z_values.at[hop - 1], device))

    attn_copy.wait()
    branch = dot(attended[...], attn[3])
    store_grid(one_out, (load_padded(one_ref, pad).astype(F32) - branch).astype(BF16))
    for part in range(3):
        inside = pl.ds(part * 256, 256)
        lhs = dot_nt(orders[part], d_query[...]).astype(BF16)
        first_full[:, pl.ds(part * 512, 256)] = dot(lhs, normed_ref[:, inside]).astype(BF16)
        lhs = dot_nt(orders[part], total_ref[...]).astype(BF16)
        first_full[:, pl.ds(part * 512 + 256, 256)] = dot(lhs, attended[:, inside]).astype(BF16)
        first.send0(part)

    for copy in copies:
        copy.wait_recv()
    total = d_keys[x].astype(F32)
    total_v = d_values[:, z].astype(F32)
    for slot in range(3):
        total = total + x_keys[slot].astype(F32)
        total_v = total_v + z_values[slot].astype(F32)
    key_sum[...] = total.astype(BF16)
    value_sum[...] = total_v.astype(BF16)
    copies = []
    for hop in (2, 1, 3):
        device, at = place.along(2, hop)
        copies.append(links.start(key_sum.at[at], z_keys.at[hop - 1], device))
        device, at = place.along(0, hop)
        copies.append(links.start(value_sum.at[at], x_values.at[hop - 1], device))
    for copy in copies:
        copy.wait_recv()
    total = key_sum[z].astype(F32)
    total_v = value_sum[x].astype(F32)
    for slot in range(3):
        total = total + z_keys[slot].astype(F32)
        total_v = total_v + x_values[slot].astype(F32)
    key_pair[...] = total.astype(BF16)
    value_pair[...] = total_v.astype(BF16)
    at_other = pl.ds(pl.multiple_of((1 - low) * 16, 16), 16)
    copies = [
        links.start(key_pair.at[at_other, :], y_keys, place.pair()),
        links.start(value_pair.at[at_other, :], y_values, place.pair()),
    ]
    for part in range(3):
        mlp.send2(part)
    for copy in copies:
        copy.wait_recv()
    d_pooled[:, 0:D] = (key_pair[at_low, :].astype(F32) + y_keys[...].astype(F32)).astype(BF16)
    d_pooled[:, D:] = (value_pair[at_low, :].astype(F32) + y_values[...].astype(F32)).astype(BF16)
    copies = [
        links.start(d_pooled, d_halo.at[0], place.frame(1)),
        links.start(d_pooled, d_halo.at[1], place.frame(-1)),
    ]
    for part in range(3):
        first.send1(part)
    for copy in copies:
        copy.wait_recv()

    from_left = jnp.where(place.tm > 0, d_halo[0].astype(F32), 0.0).astype(BF16)
    from_right = jnp.where(place.tm < 31, d_halo[1].astype(F32), 0.0).astype(BF16)
    cells, blocks = cell_maps()
    keyval = keyval_ref[...].astype(F32)
    d_keyval = None
    extra[...] = jnp.zeros(extra.shape, BF16)
    for offset, source in enumerate((from_right, d_pooled[...], from_left)):
        expanded = dot(blocks, source)
        term = spread[offset] * expanded
        d_keyval = term if d_keyval is None else d_keyval + term
        d_kernel = gather_rows(cells[:, 0:16], keyval * expanded).astype(BF16)
        extra[0, 16 * offset : 16 * offset + 16, :] = d_kernel
        extra[1, 48 + 16 * offset : 64 + 16 * offset, :] = d_kernel
    d_keyval = d_keyval.astype(BF16)
    d_key_proj, d_value_proj = d_keyval[:, 0:D], d_keyval[:, D:]

    def last_part(part):
        inside = pl.ds(part * 256, 256)
        lhs = dot_nt(orders[part], d_key_proj).astype(BF16)
        last_full[:, pl.ds(part * 512, 256)] = dot(lhs, normed_ref[:, inside]).astype(BF16)
        lhs = dot_nt(orders[part], d_value_proj).astype(BF16)
        last_full[:, pl.ds(part * 512 + 256, 256)] = dot(lhs, normed_ref[:, inside]).astype(BF16)

    for part in range(2):
        last_part(part)
        last.send0(part)
    last_part(2)
    d_normed = dot_nt(d_query[...], attn[0])
    d_normed = d_normed + dot_nt(d_key_proj, attn[1]) + dot_nt(d_value_proj, attn[2])
    unit, scale = norm_stats(load_padded(two_ref, pad).astype(F32))
    d_second = norm_back(unit, scale, gain_ref[1:2, :], d_normed)
    d_gain = jnp.sum(d_normed * unit, axis=0, keepdims=True)
    extra_gain[...] = jnp.zeros(extra_gain.shape, F32)
    extra_gain[96:97, :] = gain_one_ref[...]
    extra_gain[97:98, :] = d_gain
    source = source_column(iota((D, 128), 0), 2)
    lanes = iota((D, 128), 1)
    block = dot_nt(orders[2], extra_gain[...].astype(BF16))
    for k in range(KV // 128):
        for side in range(2):
            pick = jnp.where(2 * source + side == lanes + 128 * k, 1.0, 0.0).astype(BF16)
            block = block + dot_nt(pick, extra[side, :, k * 128 : (k + 1) * 128])
    last_full[:, pl.ds(1536, 128)] = block.astype(BF16)
    last.send0(2)
    result = load_padded(cot_two_ref, pad).astype(F32) + d_second
    store_grid(grad_two_out, result.astype(BF16))

    for part in range(3):
        first.send2(part)
    for part in range(3):
        last.send1(part)
    for part in range(3):
        mlp.send3(part)
    for part in range(3):
        first.send3(part)
    for part in range(3):
        last.send2(part)
    for part in range(3):
        mlp.finish(part)
    for part in range(3):
        last.send3(part)
    for part in range(3):
        first.finish(part)
    for part in range(3):
        last.finish(part)
    for copy in links.started:
        copy.wait_send()


def run_attention(ready, half_one, input_two, grad_two, norm_gain, pool_kernel, attn_weight, mlp_sums):
    vmem = pl.BlockSpec(memory_space=pltpu.VMEM)
    hbm = pl.BlockSpec(memory_space=pl.ANY)
    shape = jax.ShapeDtypeStruct
    scratch = [
        pltpu.SemaphoreType.DMA((N_COPIES,)),
        pltpu.SemaphoreType.DMA((N_COPIES,)),
        pltpu.SemaphoreType.DMA((4,)),
        pltpu.VMEM((HALF, MLP_COLS), BF16), *landing(MLP_COLS),
        pltpu.VMEM((D, FIRST_COLS), BF16), *landing(FIRST_COLS),
        pltpu.VMEM((D, LAST_COLS), BF16), *landing(LAST_COLS),
        pltpu.VMEM((4, D, D), BF16),
        pltpu.VMEM((3, ROWS, KV), F32),
        pltpu.VMEM((3, D, D), BF16),
        pltpu.VMEM((16, KV), F32),
        pltpu.VMEM((2, 16, KV), F32),
        pltpu.VMEM((16, KV), BF16),
        pltpu.VMEM((14, 16, D), BF16),
        *[pltpu.VMEM((4, 4, 32, D), BF16) for _ in range(4)],
        pltpu.VMEM((3, 4, 32, D), BF16),
        pltpu.VMEM((3, 32, D), BF16),
        pltpu.VMEM((16, D), BF16),
        pltpu.VMEM((3, 32, D), BF16),
        pltpu.VMEM((3, 4, 32, D), BF16),
        pltpu.VMEM((16, D), BF16),
        pltpu.VMEM((4, 32, D), BF16),
        pltpu.VMEM((4, 32, D), BF16),
        pltpu.VMEM((32, D), BF16),
        pltpu.VMEM((32, D), BF16),
        pltpu.VMEM((16, KV), BF16),
        pltpu.VMEM((2, 16, KV), BF16),
        pltpu.VMEM((ROWS, D), BF16),
        pltpu.VMEM((ROWS, D), BF16),
        pltpu.VMEM((2, 128, KV), BF16),
        pltpu.VMEM((128, D), F32),
    ]
    return pl.pallas_call(
        attention_kernel,
        in_specs=[vmem] * 12 + [hbm] * 2,
        out_specs=[vmem] * 3,
        out_shape=[
            shape(half_one.shape, BF16), shape(half_one.shape, BF16),
            shape((8, MLP_COLS + FIRST_COLS + LAST_COLS), F32),
        ],
        scratch_shapes=scratch,
        compiler_params=pltpu.CompilerParams(
            collective_id=0, has_side_effects=True, vmem_limit_bytes=62 * MIB
        ),
        name="attention_branch",
    )(*ready, half_one, input_two, grad_two, norm_gain, pool_kernel, attn_weight, mlp_sums)


def shards(half_one, half_two, grad_one, grad_two, norm_gain, attn_weight, mlp_weight, pool_kernel):
    (input_two, total, mlp_sums, normed, query, keyval, d_att, total_pad, parts, gain_one) = run_mlp(
        half_one, half_two, grad_one, grad_two, norm_gain, attn_weight, mlp_weight, pool_kernel
    )
    input_one, input_grad_two, sums = run_attention(
        (query, keyval, d_att, total_pad, normed, parts, gain_one),
        half_one, input_two, grad_two, norm_gain, pool_kernel, attn_weight, mlp_sums,
    )
    sums = sums[0:6]
    mlp_grad = sums[:, 0:MLP_COLS].reshape(6, STEPS, 2, CHUNK)
    mlp_grad = mlp_grad.transpose(2, 1, 3, 0).reshape(2, FF, 6)
    first = sums[:, MLP_COLS : MLP_COLS + FIRST_COLS].reshape(6, 3, 2, 256)
    first = first.transpose(2, 1, 3, 0).reshape(2, D, 6)
    last = sums[:, MLP_COLS + FIRST_COLS :]
    rest = last[:, 1536:]
    last = last[:, 0:1536].reshape(6, 3, 2, 256).transpose(2, 1, 3, 0).reshape(2, D, 6)
    attn_grad = jnp.concatenate([first[0:1], last, first[1:2]], axis=0)
    kernel_grad = rest[:, 0:96].reshape(6, 2, 48).transpose(2, 0, 1).reshape(3, 4, 4, 12)
    gain_grad = rest[:, 96:98].T
    return (input_one, input_two, total, input_grad_two, attn_grad, mlp_grad, kernel_grad, gain_grad)


def solution(mesh):
    placed = (
        P("clip", "tm", None, None, None),
        P("clip", "tm", None, None, None),
        P("clip", "tm", None, None, None),
        P("clip", "tm", None, None, None),
        P(),
        P(),
        P(),
        P(),
    )
    return jax.shard_map(
        shards,
        mesh=mesh,
        in_specs=placed,
        out_specs=(
            P("clip", "tm", None, None, None),
            P("clip", "tm", None, None, None),
            P("clip", "tm", None, None, None),
            P("clip", "tm", None, None, None),
            P(None, None, ("clip", "tm")),
            P(None, None, ("clip", "tm")),
            P(None, None, None, ("clip", "tm")),
            P(None, ("clip", "tm")),
        ),
        check_vma=False,
    )
```

time: 699 us -> 148 us (0.21)
  waiting for transfers between devices: 412 us -> 0 us
  Pallas kernels: 0 us -> 125 us
  blocking collectives: 89.2 us -> 0 us
  local copies, waits for them, and re-layouts: 84 us -> 20 us
  matrix products: 50.5 us -> 0 us
  other arithmetic: 34.5 us -> 0.69 us
  between operations: 14.5 us -> 0.73 us
  starting transfers between devices: 12 us -> 0 us
    unnamed x4 -> x0, waiting for transfers between devices: 161 us -> none
    pallas_call x0 -> x2, Pallas kernels: none -> 125 us  [the longest x1 106 us: run_attention(): pl.pallas_call(attention_kernel, in_specs=[vmem] * 12 + [hbm] * 2, out_sp...]
    all_gather x1 -> x0, waiting for transfers between devices: 114 us -> none  [shards(): gathered = lax.all_gather(pooled_b, 'tm', axis=1, tiled=True)]
    reduce_scatter x1 -> x0, waiting for transfers between devices: 109 us -> none  [shards(): lax.psum_scatter(d_pooled_all.astype(jnp.bfloat16), 'tm', scatter_dimensi...]
    unnamed x1 -> x0, blocking collectives: 89.2 us -> none
    dot_general x19 -> x0, matrix products: 50.5 us -> none  [the longest x1 5.64 us: shards(): lax.dot_general(cot_two_flat, mlp_weight[1], contract_last, preferred_ele...]
    another operation x3 -> x0, local copies, waits for them, and re-layouts: 41.1 us -> none  [the longest x1 28.4 us: shards(): mlp_part = jnp.stack([d_up, d_down])]
    ppermute x4 -> x0, waiting for transfers between devices: 28.3 us -> none  [the longest x2 15.6 us: extended(): lax.ppermute(lax.slice_in_dim(block, block.shape[dim] - width, None, axis...]
  transfers between devices with their start and end apart: 7 -> 0, of which waited for: 5 -> 0; matrix products, arithmetic and copies ran while one was open for 12% -> 0% of each run, Pallas kernels for 0% -> 0%
where the time goes in v1:
time: 148 us; the launch traced here: 147 us
  Pallas kernels  125 us (84%)
  local copies, waits for them, and re-layouts  20 us (14%)
    pallas_call x1, Pallas kernels, run_attention(): pl.pallas_call(attention_kernel, in_specs=[vmem] * 12 + [hbm] * 2, out_sp...  106 us
    pallas_call x1, Pallas kernels, run_mlp(): pl.pallas_call(mlp_kernel, grid=(STEPS,), in_specs=[grid_block, grid_bloc...  19.2 us
    unnamed x30, local copies, waits for them, and re-layouts  15.5 us

profile of v1, /device:TPU:1, one launch (start us, length us, event | category | flops | bytes accessed | tf_op | source)
XLA Modules:
  0.0 146.7 jit_solution(3839051312462623009)
XLA Ops:
  0.6 0.0 copy-start
  0.6 1.0 copy-done
  1.6 0.0 copy-start.1
  1.6 1.0 copy-done.1
  2.6 0.0 copy-start.2
  2.6 1.0 copy-done.2
  3.6 1.0 copy-done.8
  4.5 1.0 copy-done.9
  5.5 0.7 copy-done.11
  6.2 19.2 %mlp_branch.1 = (bf16[1,1,14,14,768]{4,3,2,1,0:T(8,128)(2,1)}, bf16[1,1,14,14,768]{4,3,2,1,0:T(8,128)(2,1)}, bf16[768,6144]{1,0:T(8,128)(2,1)}, bf16[224,768]{1,...) custom-call(bf16[1,1,14,14,768]{4,3,2,1,0:T(8,128)(2,1)S(1)} %copy-d, ...), custom_call_target="tpu_custom_call" | custom-call | tf_op jit(solution)/shard_map/mlp_branch/pallas_call | solution.py:187
  25.4 0.0 copy-start.3
  25.4 0.9 copy-done.3
  26.3 0.7 copy-done.4
  27.0 0.7 copy-done.5
  27.7 0.7 copy-done.6
  28.5 0.8 copy-done.7
  29.2 0.7 copy-done.10
  29.9 0.6 copy-done.12
  30.5 106.0 %attention_branch.1 = (bf16[1,1,14,14,768]{4,3,2,1,0:T(8,128)(2,1)}, bf16[1,1,14,14,768]{4,3,2,1,0:T(8,128)(2,1)}, f32[8,9344]{1,0:T(8,128)}) custom-call(bf16[224,768]{1,0:T(8,128)(2,1)} %copy-done.5, bf16[224,1536]{1,0:T(8,128)(2,1)} %copy-done.3, bf16[224,768]{1,0:T(8,128)(2,1)} %copy-done.6, bf16[224,768]{1,0:T(8,128)(2,1)} %copy-done.7, ...), custom_call_target="tpu_custom_call" | custom-call | tf_op jit(solution)/shard_map/attention_branch/pallas_call | solution.py:692
  136.6 0.7 slice.44
  137.3 0.1 reshape.45
  137.3 0.8 slice_bitcast_fusion
  138.1 0.7 copy.23
  138.7 0.1 reshape.46
  138.8 0.8 copy.22
  139.6 0.8 fusion
  140.4 0.9 slice.43
  141.4 0.1 reshape.43
  141.7 0.7 pad_maximum_fusion
  142.4 0.8 reshape.44
  143.2 1.7 %copy.30 = bf16[1,1,14,14,768]{4,3,2,1,0:T(8,128)(2,1)} copy(bf16[1,1,14,14,768]{4,3,2,1,0:T(8,128)(2,1)} %get-tuple-element.62) | data formatting | bytes 602112
  144.9 1.7 %copy.31 = bf16[1,1,14,14,768]{4,3,2,1,0:T(8,128)(2,1)} copy(bf16[1,1,14,14,768]{4,3,2,1,0:T(8,128)(2,1)} %get-tuple-element.65) | data formatting | bytes 602112
  (15 shorter events, 0.2 us)
Async XLA Ops:
  0.6 1.0 copy-start
  1.6 1.0 copy-start.1
  2.6 1.0 copy-start.2
  3.6 1.0 copy-start.8
  4.5 1.0 copy-start.9
  5.5 0.7 copy-start.11
  25.4 0.9 copy-start.3
  26.3 0.7 copy-start.4
  27.0 0.7 copy-start.5
  27.7 0.7 copy-start.6
  28.5 0.8 copy-start.7
  29.2 0.7 copy-start.10
  29.9 0.6 copy-start.12

commit v2 on v1

v2 whole, which is shorter than its diff:
```python
from functools import partial

import jax
import jax.numpy as jnp
from jax import lax
from jax.experimental import pallas as pl
from jax.experimental.pallas import tpu as pltpu
from jax.sharding import PartitionSpec as P

D = 768
FF = 3072
KV = 2 * D
ROWS = 224
CHUNK = 512
STEPS = FF // CHUNK
HALF = 384
MIB = 1024 * 1024
F32 = jnp.float32
BF16 = jnp.bfloat16
MESH = pl.DeviceIdType.MESH


def dot(a, b):
    return lax.dot_general(a, b, (((1,), (0,)), ((), ())), preferred_element_type=F32)


def dot_nt(a, b):
    return lax.dot_general(a, b, (((1,), (1,)), ((), ())), preferred_element_type=F32)


def dot_tn(a, b):
    return lax.dot_general(a, b, (((0,), (0,)), ((), ())), preferred_element_type=F32)


def iota(shape, dim):
    return lax.broadcasted_iota(jnp.int32, shape, dim)


def source_column(rows, part):
    owner_at = (rows * 43691) >> 18
    inner = rows - owner_at * 6
    core = owner_at >> 6
    digits = ((owner_at >> 4) & 3, (owner_at >> 2) & 3, owner_at & 3)
    x, y, z = (digits[(axis - part) % 3] for axis in range(3))
    owner = (y >> 1) * 64 + core * 32 + x * 8 + z * 2 + (y & 1)
    return owner * 6 + inner


def permutation(part):
    source = source_column(iota((D, 128), 0), part)
    lanes = iota((D, 128), 1)
    pieces = [
        jnp.where(source == lanes + 128 * k, 1.0, 0.0).astype(BF16) for k in range(D // 128)
    ]
    return jnp.concatenate(pieces, axis=1)


def norm_stats(values):
    centre = jnp.mean(values, axis=-1, keepdims=True)
    centred = values - centre
    spread = jnp.mean(centred * centred, axis=-1, keepdims=True)
    scale = lax.rsqrt(spread + 1e-05)
    return centred * scale, scale


def norm_back(unit, scale, gain, cotangent):
    d_unit = cotangent * gain
    first = jnp.mean(d_unit, axis=-1, keepdims=True)
    second = jnp.mean(d_unit * unit, axis=-1, keepdims=True)
    return scale * (d_unit - first - unit * second)


def load_padded(ref, pad):
    pad[...] = jnp.zeros(pad.shape, pad.dtype)
    pad[:, 0:14, :] = ref[0, 0]
    return pad[...].reshape(ROWS, D)


def store_grid(ref, values):
    ref[0, 0] = values.reshape(14, 16, D)[:, 0:14, :]


def cell_maps():
    row = iota((ROWS, 48), 0)
    across, down = (row & 15) + 1, (row >> 4) + 1
    valid = across < 15
    cell = (down & 3) * 4 + (across & 3)
    lane = iota((ROWS, 48), 1)
    cells = jnp.where(valid & ((lane & 15) == cell), 1.0, 0.0).astype(BF16)
    row = iota((ROWS, 16), 0)
    across, down = (row & 15) + 1, (row >> 4) + 1
    block = (down >> 2) * 4 + (across >> 2)
    blocks = jnp.where((across < 15) & (iota((ROWS, 16), 1) == block), 1.0, 0.0).astype(BF16)
    return cells, blocks


def spread_kernel(cells, flat):
    high = flat.astype(BF16)
    rest = flat - high.astype(F32)
    middle = rest.astype(BF16)
    low = (rest - middle.astype(F32)).astype(BF16)
    return dot(cells, jnp.concatenate([high, middle, low], axis=0))


def gather_rows(one_hot, values):
    high = values.astype(BF16)
    low = (values - high.astype(F32)).astype(BF16)
    return dot_tn(one_hot, high) + dot_tn(one_hot, low)


class Links:
    def __init__(self, send, recv):
        self.send, self.recv, self.used, self.started = send, recv, 0, []

    def start(self, source, target, device, shift=0, slots=1):
        copy = pltpu.make_async_remote_copy(
            src_ref=source, dst_ref=target,
            send_sem=self.send.at[self.used], recv_sem=self.recv.at[self.used + shift],
            device_id=device, device_id_type=MESH,
        )
        self.used += slots
        copy.start()
        self.started.append(copy)
        return copy

    def arrival(self, target, number):
        pltpu.make_async_remote_copy(
            src_ref=target, dst_ref=target,
            send_sem=self.send.at[number], recv_sem=self.recv.at[number],
            device_id=(lax.axis_index("clip"), lax.axis_index("tm")), device_id_type=MESH,
        ).wait_recv()

    def sent(self, copy):
        copy.wait_send()
        self.started = [other for other in self.started if other is not copy]


class Place:
    def __init__(self):
        clip, tm = lax.axis_index("clip"), lax.axis_index("tm")
        self.tm, self.clip = tm, clip
        self.core, high = clip % 2, clip // 2
        self.low = tm % 2
        self.at = (tm // 8, high * 2 + self.low, (tm // 2) % 4)

    def device(self, core, at):
        x, y, z = at
        return ((y // 2) * 2 + core, x * 8 + z * 2 + y % 2)

    def other_core(self):
        return self.device(1 - self.core, self.at)

    def along(self, axis, hop):
        at = list(self.at)
        at[axis] = (at[axis] + hop) % 4
        return self.device(self.core, at), at[axis]

    def pair(self, hop, low):
        return (self.clip, (self.tm - self.low + 2 * hop + 32) % 32 + low)


class Reduction:
    def __init__(self, links, place, parts, held, base, offset, landed, store):
        self.links, self.place, self.parts = links, place, parts
        self.held, self.base, self.offset = held, base, offset
        self.in0, self.in1, self.sum1, self.in2, self.sum2, self.in3 = landed
        self.store = store
        self.copies = {}

    def columns(self, part, offset=0):
        return pl.ds(self.parts[part][0] + offset, self.parts[part][1])

    def blocks(self, part, width=512):
        first, count = self.parts[part]
        if count % width:
            width = count
        return [(first + k * width, width) for k in range(count // width)]

    def send0(self, part):
        cols = self.columns(part)
        rows = pl.ds(pl.multiple_of((1 - self.place.core) * HALF, HALF), HALF)
        self.copies[0, part] = [
            self.links.start(
                self.held.at[rows, self.columns(part, self.offset)], self.in0.at[:, cols],
                self.place.other_core(),
            )
        ]

    def arrive(self, stage, part):
        for copy in self.copies[stage, part]:
            copy.wait_recv()

    def spread(self, stage, part, source, base, offset, rows, target):
        axis = (part + stage - 1) % 3
        cols = self.columns(part)
        source_cols = self.columns(part, offset)
        self.copies[stage, part] = []
        for hop in (2, 1, 3):
            device, at = self.place.along(axis, hop)
            window = pl.ds(pl.multiple_of(base + at * rows, rows), rows)
            self.copies[stage, part].append(
                self.links.start(
                    source.at[window, source_cols], target.at[hop - 1, :, cols], device
                )
            )

    def send1(self, part):
        self.arrive(0, part)
        first, count = self.parts[part]

        def body(k, carry):
            rows = pl.ds(pl.multiple_of(k * 16, 16), 16)
            mine = pl.ds(pl.multiple_of(self.base + k * 16, 16), 16)
            cols, held_cols = pl.ds(first, count), pl.ds(first + self.offset, count)
            total = self.held[mine, held_cols].astype(F32) + self.in0[rows, cols].astype(F32)
            self.held[mine, held_cols] = total.astype(BF16)
            return carry

        lax.fori_loop(0, HALF // 16, body, 0)
        self.spread(1, part, self.held, self.base, self.offset, 96, self.in1)

    def send2(self, part):
        self.arrive(1, part)
        mine = self.place.at[part % 3]
        rows = pl.ds(pl.multiple_of(self.base + mine * 96, 96), 96)
        place_row, place_col = iota((128, 96), 0), iota((128, 96), 1)
        owner = place_row >> 3
        inner = place_row & 7
        widen = jnp.where((inner < 6) & (place_col == owner * 6 + inner), 1.0, 0.0).astype(BF16)
        for first, count in self.blocks(part):
            cols = pl.ds(first, count)
            total = self.held[rows, pl.ds(first + self.offset, count)].astype(F32)
            for slot in range(3):
                total = total + self.in1[slot, :, cols].astype(F32)
            self.sum1[:, cols] = dot(widen, total.astype(BF16)).astype(BF16)
        self.spread(2, part, self.sum1, 0, 0, 32, self.in2)

    def send3(self, part):
        self.arrive(2, part)
        mine = self.place.at[(part + 1) % 3]
        rows = pl.ds(pl.multiple_of(mine * 32, 32), 32)
        for first, count in self.blocks(part):
            cols = pl.ds(first, count)
            total = self.sum1[rows, cols].astype(F32)
            for slot in range(3):
                total = total + self.in2[slot, :, cols].astype(F32)
            self.sum2[:, cols] = total
        self.spread(3, part, self.sum2, 0, 0, 8, self.in3)

    def finish(self, part):
        self.arrive(3, part)
        mine = self.place.at[(part + 2) % 3]
        rows = pl.ds(pl.multiple_of(mine * 8, 8), 8)
        for first, count in self.blocks(part):
            cols = pl.ds(first, count)
            total = self.sum2[rows, cols]
            for slot in range(3):
                total = total + self.in3[slot, :, cols]
            self.store(part, (first - self.parts[part][0]) // 512, total)


MLP_PARTS = tuple((p * 2048, 2048) for p in range(3))
FIRST_PARTS = tuple((p * 512, 512) for p in range(3))
LAST_PARTS = ((0, 512), (512, 512), (1024, 640))
MLP_COLS, FIRST_COLS, LAST_COLS = 6144, 1536, 1664
CHUNK_ORDER = (0, 1, 4, 5, 2, 3)
N_COPIES = 6 + 3 * 9 + 2 * 30 + 6 + 12 + 18 + 6


def landing(cols):
    return [
        pltpu.VMEM((HALF, cols), BF16),
        pltpu.VMEM((3, 96, cols), BF16),
        pltpu.VMEM((128, cols), BF16),
        pltpu.VMEM((3, 32, cols), BF16),
        pltpu.VMEM((32, cols), F32),
        pltpu.VMEM((3, 8, cols), F32),
    ]


def block_kernel(
    one_hbm, two_hbm, cot_one_hbm, cot_two_hbm, gain_ref, attn_hbm, mlp_hbm, pool_hbm,
    one_out, two_out, total_out, grad_two_out, mlp_out, attn_out, rest_out,
    *scratch,
):
    scratch = list(scratch)

    def take(count):
        taken = scratch[:count]
        del scratch[:count]
        return taken

    send_sem, recv_sem, local_sem, weight_sem = take(4)
    one_in, two_in, cot_one_in, cot_two_in, pool_in = take(5)
    up_buf, down_buf, stage = take(3)
    mlp_own, mlp_land = take(1)[0], take(6)
    first_land, last_land = take(6), take(6)
    attn, orders, pool, pad = take(4)
    normed, cot, branch, d_normed = take(4)
    normed_two, query, keyval, d_att, total, lefts = take(6)
    parts, from_pair, from_edge = take(3)
    keys, values, d_keys, d_values = take(4)
    x_keys, z_keys, x_values, z_values = take(4)
    key_sum, value_sum, pair_sum, pair_land, edge_land = take(5)
    attended, d_query, extra, extra_gain = take(4)

    place = Place()
    links = Links(send_sem, recv_sem)
    x, y, z = place.at
    low = place.low

    sources = (one_hbm, cot_two_hbm, two_hbm, cot_one_hbm, pool_hbm, attn_hbm)
    targets = (one_in, cot_two_in, two_in, cot_one_in, pool_in, attn)
    fetches = [
        pltpu.make_async_copy(source, target, local_sem.at[k])
        for k, (source, target) in enumerate(zip(sources, targets))
    ]
    one_copy, cot_two_copy, two_copy, cot_one_copy, pool_copy, attn_copy = fetches

    def weight_copies(k):
        rows = pl.ds(CHUNK_ORDER[k] * CHUNK, CHUNK)
        return [
            pltpu.make_async_copy(mlp_hbm.at[0, rows], up_buf.at[k % 2], weight_sem.at[0, k % 2]),
            pltpu.make_async_copy(mlp_hbm.at[1, rows], down_buf.at[k % 2], weight_sem.at[1, k % 2]),
        ]

    one_copy.start()
    cot_two_copy.start()
    for k in range(2):
        for copy in weight_copies(k):
            copy.start()
    for copy in fetches[2:]:
        copy.start()

    barrier = pltpu.get_barrier_semaphore()
    partners = [place.other_core()]
    partners += [place.pair(hop, side) for hop in (-1, 1) for side in range(2)]
    partners += [place.along(axis, hop)[0] for axis in range(3) for hop in (1, 2, 3)]
    for device in partners:
        pl.semaphore_signal(barrier, inc=1, device_id=device, device_id_type=MESH)

    def store_mlp(part, block, values):
        at = pl.ds((2 * part + block // 2) * CHUNK, CHUNK)
        mlp_out[:, block % 2, at] = values[0:6]

    def store_first(part, block, values):
        at = pl.ds(part * 256, 256)
        attn_out[:, 0, at] = values[0:6, 0:256]
        attn_out[:, 3, at] = values[0:6, 256:512]

    def store_last(part, block, values):
        at = pl.ds(part * 256, 256)
        attn_out[:, 1, at] = values[0:6, 0:256]
        attn_out[:, 2, at] = values[0:6, 256:512]
        if part == 2:
            rest_out[...] = values[:, 512:640]

    own_base = pl.multiple_of(place.core * HALF, HALF)
    other_base = pl.multiple_of((1 - place.core) * HALF, HALF)
    mlp = Reduction(links, place, MLP_PARTS, mlp_own, 0, 0, mlp_land, store_mlp)
    first = Reduction(links, place, FIRST_PARTS, stage, own_base, 0, first_land, store_first)
    last = Reduction(links, place, LAST_PARTS, stage, own_base, FIRST_COLS, last_land, store_last)

    one_copy.wait()
    unit, scale = norm_stats(load_padded(one_in, pad).astype(F32))
    normed[...] = (unit * gain_ref[0:1, :]).astype(BF16)
    cot_two_copy.wait()
    cot[...] = load_padded(cot_two_in, pad)
    for k, chunk in enumerate(CHUNK_ORDER):
        part = chunk // 2
        if chunk % 2 == 0:
            orders[part] = permutation(part)
            lefts[0] = dot_nt(orders[part], normed[...]).astype(BF16)
            lefts[1] = dot_nt(orders[part], cot[...]).astype(BF16)
        for copy in weight_copies(k):
            copy.wait()
        up, down = up_buf[k % 2], down_buf[k % 2]
        hidden = dot_nt(normed[...], up)
        inner = 0.7978845608028654 * (hidden + 0.044715 * hidden * hidden * hidden)
        tanh = jnp.tanh(inner)
        half_sum = 0.5 * (1.0 + tanh)
        active = (hidden * half_sum).astype(BF16)
        slope = half_sum + 0.5 * hidden * (1.0 - tanh * tanh) * (
            0.7978845608028654 * (1.0 + 3.0 * 0.044715 * hidden * hidden)
        )
        d_hidden = (slope * dot_nt(cot[...], down)).astype(BF16)
        if k == 0:
            branch[...] = dot(active, down)
            d_normed[...] = dot(d_hidden, up)
        else:
            branch[...] += dot(active, down)
            d_normed[...] += dot(d_hidden, up)
        if k + 2 < STEPS:
            for copy in weight_copies(k + 2):
                copy.start()
        at = (chunk % 2) * HALF
        cols = part * 2 * CHUNK
        for side, values_in in enumerate((d_hidden, active)):
            rows = pl.ds(other_base, HALF)
            stage[pl.ds(at, HALF), pl.ds(cols + side * CHUNK, CHUNK)] = dot(
                lefts[side, rows], values_in
            ).astype(BF16)
        if k == 0:
            pl.semaphore_wait(barrier, len(partners))
        mlp.copies.setdefault((0, part), []).append(
            links.start(
                stage.at[pl.ds(at, HALF), pl.ds(cols, 2 * CHUNK)],
                mlp.in0.at[:, pl.ds(chunk * 2 * CHUNK, 2 * CHUNK)],
                place.other_core(),
            )
        )
        for side, values_in in enumerate((d_hidden, active)):
            rows = pl.ds(own_base, HALF)
            mlp_own[:, pl.ds(chunk * 2 * CHUNK + side * CHUNK, CHUNK)] = dot(
                lefts[side, rows], values_in
            ).astype(BF16)
        if k == 2:
            mlp.send1(0)
        if k == 4:
            mlp.send1(2)

    two_copy.wait()
    restored = (load_padded(two_in, pad).astype(F32) - branch[...]).astype(BF16)
    store_grid(two_out, restored)
    unit_two, scale_two = norm_stats(restored.astype(F32))
    normed_two[...] = (unit_two * gain_ref[1:2, :]).astype(BF16)
    attn_copy.wait()
    keyval[:, 0:D] = dot(normed_two[...], attn[1]).astype(BF16)
    keyval[:, D:] = dot(normed_two[...], attn[2]).astype(BF16)
    cells, blocks = cell_maps()
    pool_copy.wait()
    for offset in range(3):
        for i in range(4):
            pool[offset, 4 * i : 4 * i + 4, :] = pool_in[offset, i]
        weighted = spread_kernel(cells, pool[offset]) * keyval[...].astype(F32)
        parts[2 - offset] = gather_rows(blocks, weighted).astype(BF16)

    mine = pl.ds(1 - low, 2)
    pair_copy = links.start(parts.at[mine], from_pair, place.pair(0, 1 - low))
    edge_base = links.used
    for side in range(2):
        links.start(
            parts.at[2 * low], from_edge.at[1 - low],
            (place.clip, (place.tm - low + 4 * low - 2 + 32) % 32 + side),
            shift=1 - low if side == 0 else -low, slots=1,
        )
    mlp.send1(1)
    query[...] = dot(normed_two[...], attn[0]).astype(BF16)
    back = d_normed[...]
    unit, scale = norm_stats(load_padded(one_in, pad).astype(F32))
    d_gain_one = jnp.sum(back * unit, axis=0, keepdims=True)
    d_first = norm_back(unit, scale, gain_ref[0:1, :], back)
    cot_one_copy.wait()
    total[...] = (load_padded(cot_one_in, pad).astype(F32) + d_first).astype(BF16)
    store_grid(total_out, total[...])
    pair_copy.wait_recv()
    for slot in range(2):
        links.arrival(from_edge.at[slot], edge_base + slot)
    ends = (place.tm // 2 > 0, place.tm // 2 < 15)
    for slot in range(2):
        edge = jnp.where(ends[slot], from_edge[slot].astype(F32), 0.0)
        frame = parts[1 - low + slot].astype(F32) + from_pair[slot].astype(F32) + edge
        frame = frame.astype(BF16)
        keys[x, z, 16 * slot : 16 * slot + 16, :] = frame[:, 0:D]
        values[x, z, 16 * slot : 16 * slot + 16, :] = frame[:, D:]

    copies = []
    for hop in (2, 1, 3):
        copies.append(links.start(keys.at[x, z], keys.at[x, z], place.along(2, hop)[0]))
        copies.append(links.start(values.at[x, z], values.at[x, z], place.along(0, hop)[0]))
    d_att[...] = dot_nt(total[...], attn[3]).astype(BF16)
    for copy in copies:
        copy.wait_recv()
    copies = []
    for hop in (2, 1, 3):
        copies.append(links.start(keys.at[x], keys.at[x], place.along(0, hop)[0]))
        copies.append(links.start(values.at[:, z], values.at[:, z], place.along(2, hop)[0]))
    for part in range(3):
        lefts[part] = dot_nt(orders[part], total[...]).astype(BF16)
    for copy in copies:
        copy.wait_recv()

    def heads(pair, carry):
        lanes = pl.ds(pl.multiple_of(pair * 128, 128), 128)
        query_pair = query[:, lanes]
        d_att_pair = d_att[:, lanes]
        key = keys[:, :, :, lanes].reshape(512, 128)
        value = values[:, :, :, lanes].reshape(512, 128)
        att = d_q = d_k = d_v = None
        for side in range(2):

            def only(array):
                lane = iota(array.shape, 1)
                keep = lane < 64 if side == 0 else lane >= 64
                return jnp.where(keep, array, jnp.zeros_like(array))

            query_h, d_att_h = only(query_pair), only(d_att_pair)
            weights = jnp.exp(dot_nt(query_h, key) * 0.125)
            probs = weights * (1.0 / jnp.sum(weights, axis=-1, keepdims=True))
            probs_b = probs.astype(BF16)
            d_probs = dot_nt(d_att_h, value)
            product = probs * d_probs
            d_scores = (product - probs * jnp.sum(product, axis=-1, keepdims=True)).astype(BF16)
            terms = (
                dot(probs_b, only(value)), dot(d_scores, only(key)),
                dot_tn(d_scores, query_h), dot_tn(probs_b, d_att_h),
            )
            if side == 0:
                att, d_q, d_k, d_v = terms
            else:
                att, d_q, d_k, d_v = (a + b for a, b in zip((att, d_q, d_k, d_v), terms))
        attended[:, lanes] = att.astype(BF16)
        d_query[:, lanes] = (d_q * 0.125).astype(BF16)
        d_keys[:, :, :, lanes] = (d_k * 0.125).astype(BF16).reshape(4, 4, 32, 128)
        d_values[:, :, :, lanes] = d_v.astype(BF16).reshape(4, 4, 32, 128)
        return carry

    copies = []
    for group in range(2):
        lax.fori_loop(3 * group, 3 * group + 3, heads, 0)
        lanes = pl.ds(group * HALF, HALF)
        for hop in (2, 1, 3):
            device, at = place.along(0, hop)
            copies.append(
                links.start(d_keys.at[at, :, :, lanes], x_keys.at[hop - 1, :, :, lanes], device)
            )
            device, at = place.along(2, hop)
            copies.append(
                links.start(d_values.at[:, at, :, lanes], z_values.at[hop - 1, :, :, lanes], device)
            )

    for part in (0, 2):
        mlp.send2(part)
    for part in range(3):
        for copy in mlp.copies[0, part]:
            links.sent(copy)
    branch_f = dot(attended[...], attn[3])
    store_grid(one_out, (load_padded(one_in, pad).astype(F32) - branch_f).astype(BF16))
    for part in range(3):
        inside = pl.ds(part * 256, 256)
        lhs = dot_nt(orders[part], d_query[...]).astype(BF16)
        stage[:, pl.ds(part * 512, 256)] = dot(lhs, normed_two[:, inside]).astype(BF16)
        stage[:, pl.ds(part * 512 + 256, 256)] = dot(
            lefts[part], attended[:, inside]
        ).astype(BF16)
        first.send0(part)
    d_normed[...] = dot_nt(d_query[...], attn[0])

    for copy in copies:
        copy.wait_recv()
    sum_k = d_keys[x].astype(F32)
    sum_v = d_values[:, z].astype(F32)
    for slot in range(3):
        sum_k = sum_k + x_keys[slot].astype(F32)
        sum_v = sum_v + z_values[slot].astype(F32)
    key_sum[...] = sum_k.astype(BF16)
    value_sum[...] = sum_v.astype(BF16)
    copies = []
    for hop in (2, 1, 3):
        device, at = place.along(2, hop)
        copies.append(links.start(key_sum.at[at], z_keys.at[hop - 1], device))
        device, at = place.along(0, hop)
        copies.append(links.start(value_sum.at[at], x_values.at[hop - 1], device))
    mlp.send2(1)
    for copy in copies:
        copy.wait_recv()
    sum_k = key_sum[z].astype(F32)
    sum_v = value_sum[x].astype(F32)
    for slot in range(3):
        sum_k = sum_k + z_keys[slot].astype(F32)
        sum_v = sum_v + x_values[slot].astype(F32)
    pair_sum[:, 0:D] = sum_k.astype(BF16)
    pair_sum[:, D:] = sum_v.astype(BF16)

    pair_copy = links.start(pair_sum, pair_land, place.pair(0, 1 - low))
    edge_base = links.used
    for hop, rows in ((-1, pl.ds(0, 16)), (1, pl.ds(16, 16))):
        side = 1 if hop == -1 else 0
        links.start(
            pair_sum.at[rows, :], edge_land.at[low], place.pair(hop, side),
            shift=low if hop == -1 else low - 1, slots=1,
        )
    for part in range(3):
        first.send1(part)
    pair_copy.wait_recv()
    for slot in range(2):
        links.arrival(edge_land.at[slot], edge_base + slot)
    edge = edge_land[0].astype(F32) + edge_land[1].astype(F32)
    inside = (low == 0) & (place.tm > 0) | (low == 1) & (place.tm < 31)
    edge = jnp.where(inside, edge, 0.0).astype(BF16)
    pair_frames = (pair_sum[...].astype(F32) + pair_land[...].astype(F32)).astype(BF16)
    frame_0, frame_1 = pair_frames[0:16, :], pair_frames[16:32, :]
    before = jnp.where(low == 0, edge, frame_0)
    here = jnp.where(low == 0, frame_0, frame_1)
    after = jnp.where(low == 0, frame_1, edge)

    cells, blocks = cell_maps()
    keyval_f = keyval[...].astype(F32)
    d_keyval = None
    extra[...] = jnp.zeros(extra.shape, BF16)
    for offset, source in enumerate((after, here, before)):
        expanded = dot(blocks, source)
        term = spread_kernel(cells, pool[offset]) * expanded
        d_keyval = term if d_keyval is None else d_keyval + term
        d_kernel = gather_rows(cells[:, 0:16], keyval_f * expanded).astype(BF16)
        extra[0, 16 * offset : 16 * offset + 16, :] = d_kernel
        extra[1, 48 + 16 * offset : 64 + 16 * offset, :] = d_kernel
    d_keyval = d_keyval.astype(BF16)
    d_key_proj, d_value_proj = d_keyval[:, 0:D], d_keyval[:, D:]

    def last_part(part):
        inside = pl.ds(part * 256, 256)
        start = FIRST_COLS + part * 512
        lhs = dot_nt(orders[part], d_key_proj).astype(BF16)
        stage[:, pl.ds(start, 256)] = dot(lhs, normed_two[:, inside]).astype(BF16)
        lhs = dot_nt(orders[part], d_value_proj).astype(BF16)
        stage[:, pl.ds(start + 256, 256)] = dot(lhs, normed_two[:, inside]).astype(BF16)

    for part in range(2):
        last_part(part)
        last.send0(part)
    last_part(2)
    d_normed_two = d_normed[...] + dot_nt(d_key_proj, attn[1]) + dot_nt(d_value_proj, attn[2])
    d_second = norm_back(unit_two, scale_two, gain_ref[1:2, :], d_normed_two)
    extra_gain[...] = jnp.zeros(extra_gain.shape, F32)
    extra_gain[96:97, :] = d_gain_one
    extra_gain[97:98, :] = jnp.sum(d_normed_two * unit_two, axis=0, keepdims=True)
    source = source_column(iota((D, 128), 0), 2)
    lanes = iota((D, 128), 1)
    block = dot_nt(orders[2], extra_gain[...].astype(BF16))
    for k in range(KV // 128):
        for side in range(2):
            pick = jnp.where(2 * source + side == lanes + 128 * k, 1.0, 0.0).astype(BF16)
            block = block + dot_nt(pick, extra[side, :, k * 128 : (k + 1) * 128])
    stage[:, pl.ds(FIRST_COLS + 1536, 128)] = block.astype(BF16)
    last.send0(2)
    result = load_padded(cot_two_in, pad).astype(F32) + d_second
    store_grid(grad_two_out, result.astype(BF16))

    for part in range(3):
        first.send2(part)
    for part in range(3):
        last.send1(part)
    for part in range(3):
        mlp.send3(part)
    for part in range(3):
        first.send3(part)
    for part in range(3):
        last.send2(part)
    for part in range(3):
        mlp.finish(part)
    for part in range(3):
        last.send3(part)
    for part in range(3):
        first.finish(part)
    for part in range(3):
        last.finish(part)
    for copy in links.started:
        copy.wait_send()


def run_block(half_one, half_two, grad_one, grad_two, norm_gain, attn_weight, mlp_weight, pool_kernel):
    vmem = pl.BlockSpec(memory_space=pltpu.VMEM)
    hbm = pl.BlockSpec(memory_space=pl.ANY)
    shape = jax.ShapeDtypeStruct
    scratch = [
        pltpu.SemaphoreType.DMA((N_COPIES,)),
        pltpu.SemaphoreType.DMA((N_COPIES,)),
        pltpu.SemaphoreType.DMA((6,)),
        pltpu.SemaphoreType.DMA((2, 2)),
        *[pltpu.VMEM((1, 1, 14, 14, D), BF16) for _ in range(4)],
        pltpu.VMEM((3, 4, 4, KV), F32),
        pltpu.VMEM((2, CHUNK, D), BF16),
        pltpu.VMEM((2, CHUNK, D), BF16),
        pltpu.VMEM((D, FIRST_COLS + LAST_COLS), BF16),
        pltpu.VMEM((HALF, MLP_COLS), BF16), *landing(MLP_COLS),
        *landing(FIRST_COLS),
        *landing(LAST_COLS),
        pltpu.VMEM((4, D, D), BF16),
        pltpu.VMEM((3, D, D), BF16),
        pltpu.VMEM((3, 16, KV), F32),
        pltpu.VMEM((14, 16, D), BF16),
        pltpu.VMEM((ROWS, D), BF16),
        pltpu.VMEM((ROWS, D), BF16),
        pltpu.VMEM((ROWS, D), F32),
        pltpu.VMEM((ROWS, D), F32),
        pltpu.VMEM((ROWS, D), BF16),
        pltpu.VMEM((ROWS, D), BF16),
        pltpu.VMEM((ROWS, KV), BF16),
        pltpu.VMEM((ROWS, D), BF16),
        pltpu.VMEM((ROWS, D), BF16),
        pltpu.VMEM((3, D, ROWS), BF16),
        pltpu.VMEM((3, 16, KV), BF16),
        pltpu.VMEM((2, 16, KV), BF16),
        pltpu.VMEM((2, 16, KV), BF16),
        *[pltpu.VMEM((4, 4, 32, D), BF16) for _ in range(4)],
        pltpu.VMEM((3, 4, 32, D), BF16),
        pltpu.VMEM((3, 32, D), BF16),
        pltpu.VMEM((3, 32, D), BF16),
        pltpu.VMEM((3, 4, 32, D), BF16),
        pltpu.VMEM((4, 32, D), BF16),
        pltpu.VMEM((4, 32, D), BF16),
        pltpu.VMEM((32, KV), BF16),
        pltpu.VMEM((32, KV), BF16),
        pltpu.VMEM((2, 16, KV), BF16),
        pltpu.VMEM((ROWS, D), BF16),
        pltpu.VMEM((ROWS, D), BF16),
        pltpu.VMEM((2, 128, KV), BF16),
        pltpu.VMEM((128, D), F32),
    ]
    return pl.pallas_call(
        block_kernel,
        in_specs=[hbm, hbm, hbm, hbm, vmem, hbm, hbm, hbm],
        out_specs=[vmem] * 7,
        out_shape=[
            *[shape(half_one.shape, BF16) for _ in range(4)],
            shape((6, 2, FF), F32), shape((6, 4, D), F32), shape((8, 128), F32),
        ],
        scratch_shapes=scratch,
        compiler_params=pltpu.CompilerParams(
            collective_id=0, has_side_effects=True, vmem_limit_bytes=63 * MIB
        ),
        name="reversible_block",
    )(half_one, half_two, grad_one, grad_two, norm_gain, attn_weight, mlp_weight, pool_kernel)


def shards(half_one, half_two, grad_one, grad_two, norm_gain, attn_weight, mlp_weight, pool_kernel):
    input_one, input_two, total, input_grad_two, mlp_sums, attn_sums, rest = run_block(
        half_one, half_two, grad_one, grad_two, norm_gain, attn_weight, mlp_weight, pool_kernel
    )
    mlp_grad = mlp_sums.transpose(1, 2, 0)
    attn_grad = attn_sums.transpose(1, 2, 0)
    kernel_grad = rest[0:6, 0:96].reshape(6, 2, 48).transpose(2, 0, 1).reshape(3, 4, 4, 12)
    gain_grad = rest[0:6, 96:98].T
    return (input_one, input_two, total, input_grad_two, attn_grad, mlp_grad, kernel_grad, gain_grad)


def solution(mesh):
    placed = (
        P("clip", "tm", None, None, None),
        P("clip", "tm", None, None, None),
        P("clip", "tm", None, None, None),
        P("clip", "tm", None, None, None),
        P(),
        P(),
        P(),
        P(),
    )
    return jax.shard_map(
        shards,
        mesh=mesh,
        in_specs=placed,
        out_specs=(
            P("clip", "tm", None, None, None),
            P("clip", "tm", None, None, None),
            P("clip", "tm", None, None, None),
            P("clip", "tm", None, None, None),
            P(None, None, ("clip", "tm")),
            P(None, None, ("clip", "tm")),
            P(None, None, None, ("clip", "tm")),
            P(None, ("clip", "tm")),
        ),
        check_vma=False,
    )
```

time: 148 us -> 127 us (0.86)
  Pallas kernels: 125 us -> 113 us
  local copies, waits for them, and re-layouts: 20 us -> 13 us
    pallas_call x2 -> x1, Pallas kernels: 125 us -> 113 us  [run_block(): pl.pallas_call(block_kernel, in_specs=[hbm, hbm, hbm, hbm, vmem, hbm, hbm...]
    unnamed x30 -> x8, local copies, waits for them, and re-layouts: 15.5 us -> 11.4 us
    slice x4 -> x0, local copies, waits for them, and re-layouts: 2.48 us -> none  [the longest x1 0.94 us: shards(): mlp_grad = sums[:, 0:MLP_COLS].reshape(6, STEPS, 2, CHUNK)]
where the time goes in v2:
time: 127 us; the launch traced here: 126 us
  Pallas kernels  113 us (89%)
  local copies, waits for them, and re-layouts  13 us (10%)
    pallas_call x1, Pallas kernels, run_block(): pl.pallas_call(block_kernel, in_specs=[hbm, hbm, hbm, hbm, vmem, hbm, hbm...  113 us
    unnamed x8, local copies, waits for them, and re-layouts  11.4 us

profile of v2, /device:TPU:1, one launch (start us, length us, event | category | flops | bytes accessed | tf_op | source)
XLA Modules:
  0.0 126.4 jit_solution(7517682490572926178)
XLA Ops:
  0.6 112.7 %reversible_block.1 = (bf16[1,1,14,14,768]{4,3,2,1,0:T(8,128)(2,1)}, bf16[1,1,14,14,768]{4,3,2,1,0:T(8,128)(2,1)}, bf16[1,1,14,14,768]{4,3,2,1,0:T(8,128)(2,1)},...) custom-call(bf16[1,1,14,14,768]{4,3,2,1,0:T(8,128)(2,1)} %one_hbm.1, ...), custom_call_target="tpu_custom_call" | custom-call | tf_op jit(solution)/shard_map/reversible_block/pallas_call | solution.py:711
  113.3 0.8 reshape.22
  114.1 0.1 reshape.23
  114.2 0.8 copy.18
  115.0 0.8 slice_bitcast_fusion
  115.7 0.7 copy.19
  116.4 1.7 %copy.26 = bf16[1,1,14,14,768]{4,3,2,1,0:T(8,128)(2,1)} copy(bf16[1,1,14,14,768]{4,3,2,1,0:T(8,128)(2,1)} %get-tuple-element.46) | data formatting | bytes 602112
  118.1 1.7 %copy.27 = bf16[1,1,14,14,768]{4,3,2,1,0:T(8,128)(2,1)} copy(bf16[1,1,14,14,768]{4,3,2,1,0:T(8,128)(2,1)} %get-tuple-element.47) | data formatting | bytes 602112
  119.8 1.7 %copy.28 = bf16[1,1,14,14,768]{4,3,2,1,0:T(8,128)(2,1)} copy(bf16[1,1,14,14,768]{4,3,2,1,0:T(8,128)(2,1)} %get-tuple-element.48) | data formatting | bytes 602112
  121.5 1.7 %copy.29 = bf16[1,1,14,14,768]{4,3,2,1,0:T(8,128)(2,1)} copy(bf16[1,1,14,14,768]{4,3,2,1,0:T(8,128)(2,1)} %get-tuple-element.49) | data formatting | bytes 602112
  123.3 1.5 %copy.30 = f32[4,768,6]{1,0,2:T(4,128)} copy(f32[4,768,6]{1,0,2:T(4,128)} %bitcast.9) | data formatting | bytes 147456
  124.8 1.6 %copy.31 = f32[2,3072,6]{1,0,2:T(2,128)} copy(f32[2,3072,6]{1,0,2:T(2,128)} %bitcast.8) | data formatting | bytes 294912

commit v3 on v2

--- a/solution.py
+++ b/solution.py
@@ -303,6 +303,7 @@
     x_keys, z_keys, x_values, z_values = take(4)
     key_sum, value_sum, pair_sum, pair_land, edge_land = take(5)
     attended, d_query, extra, extra_gain = take(4)
+    mlp_sums, attn_sums, rest_sums, out_sem = take(4)
 
     place = Place()
     links = Links(send_sem, recv_sem)
@@ -339,21 +340,28 @@
     for device in partners:
         pl.semaphore_signal(barrier, inc=1, device_id=device, device_id_type=MESH)
 
+    writes = []
+
+    def write(source, target):
+        copy = pltpu.make_async_copy(source, target, out_sem.at[len(writes)])
+        copy.start()
+        writes.append(copy)
+
     def store_mlp(part, block, values):
         at = pl.ds((2 * part + block // 2) * CHUNK, CHUNK)
-        mlp_out[:, block % 2, at] = values[0:6]
+        mlp_sums[:, block % 2, at] = values[0:6]
 
     def store_first(part, block, values):
         at = pl.ds(part * 256, 256)
-        attn_out[:, 0, at] = values[0:6, 0:256]
-        attn_out[:, 3, at] = values[0:6, 256:512]
+        attn_sums[:, 0, at] = values[0:6, 0:256]
+        attn_sums[:, 3, at] = values[0:6, 256:512]
 
     def store_last(part, block, values):
         at = pl.ds(part * 256, 256)
-        attn_out[:, 1, at] = values[0:6, 0:256]
-        attn_out[:, 2, at] = values[0:6, 256:512]
+        attn_sums[:, 1, at] = values[0:6, 0:256]
+        attn_sums[:, 2, at] = values[0:6, 256:512]
         if part == 2:
-            rest_out[...] = values[:, 512:640]
+            rest_sums[...] = values[:, 512:640]
 
     own_base = pl.multiple_of(place.core * HALF, HALF)
     other_base = pl.multiple_of((1 - place.core) * HALF, HALF)
@@ -421,7 +429,8 @@
 
     two_copy.wait()
     restored = (load_padded(two_in, pad).astype(F32) - branch[...]).astype(BF16)
-    store_grid(two_out, restored)
+    store_grid(two_in, restored)
+    write(two_in, two_out)
     unit_two, scale_two = norm_stats(restored.astype(F32))
     normed_two[...] = (unit_two * gain_ref[1:2, :]).astype(BF16)
     attn_copy.wait()
@@ -452,7 +461,8 @@
     d_first = norm_back(unit, scale, gain_ref[0:1, :], back)
     cot_one_copy.wait()
     total[...] = (load_padded(cot_one_in, pad).astype(F32) + d_first).astype(BF16)
-    store_grid(total_out, total[...])
+    store_grid(cot_one_in, total[...])
+    write(cot_one_in, total_out)
     pair_copy.wait_recv()
     for slot in range(2):
         links.arrival(from_edge.at[slot], edge_base + slot)
@@ -535,7 +545,8 @@
         for copy in mlp.copies[0, part]:
             links.sent(copy)
     branch_f = dot(attended[...], attn[3])
-    store_grid(one_out, (load_padded(one_in, pad).astype(F32) - branch_f).astype(BF16))
+    store_grid(one_in, (load_padded(one_in, pad).astype(F32) - branch_f).astype(BF16))
+    write(one_in, one_out)
     for part in range(3):
         inside = pl.ds(part * 256, 256)
         lhs = dot_nt(orders[part], d_query[...]).astype(BF16)
@@ -635,7 +646,8 @@
     stage[:, pl.ds(FIRST_COLS + 1536, 128)] = block.astype(BF16)
     last.send0(2)
     result = load_padded(cot_two_in, pad).astype(F32) + d_second
-    store_grid(grad_two_out, result.astype(BF16))
+    store_grid(cot_two_in, result.astype(BF16))
+    write(cot_two_in, grad_two_out)
 
     for part in range(3):
         first.send2(part)
@@ -649,14 +661,19 @@
         last.send2(part)
     for part in range(3):
         mlp.finish(part)
+    write(mlp_sums, mlp_out)
     for part in range(3):
         last.send3(part)
     for part in range(3):
         first.finish(part)
     for part in range(3):
         last.finish(part)
+    write(attn_sums, attn_out)
+    write(rest_sums, rest_out)
     for copy in links.started:
         copy.wait_send()
+    for copy in writes:
+        copy.wait()
 
 
 def run_block(half_one, half_two, grad_one, grad_two, norm_gain, attn_weight, mlp_weight, pool_kernel):
@@ -707,11 +724,15 @@
         pltpu.VMEM((ROWS, D), BF16),
         pltpu.VMEM((2, 128, KV), BF16),
         pltpu.VMEM((128, D), F32),
+        pltpu.VMEM((6, 2, FF), F32),
+        pltpu.VMEM((6, 4, D), F32),
+        pltpu.VMEM((8, 128), F32),
+        pltpu.SemaphoreType.DMA((7,)),
     ]
     return pl.pallas_call(
         block_kernel,
         in_specs=[hbm, hbm, hbm, hbm, vmem, hbm, hbm, hbm],
-        out_specs=[vmem] * 7,
+        out_specs=[hbm] * 7,
         out_shape=[
             *[shape(half_one.shape, BF16) for _ in range(4)],
             shape((6, 2, FF), F32), shape((6, 4, D), F32), shape((8, 128), F32),
@@ -724,14 +745,59 @@
     )(half_one, half_two, grad_one, grad_two, norm_gain, attn_weight, mlp_weight, pool_kernel)
 
 
+def hand_out_kernel(*refs):
+    taken, rest_ref, given, kernel_out, gain_out, sem = refs[0:6], refs[6], refs[7:13], *refs[13:]
+    copies = [
+        pltpu.make_async_copy(source, target, sem.at[k])
+        for k, (source, target) in enumerate(zip(taken, given))
+    ]
+    for copy in copies:
+        copy.start()
+    rest = rest_ref[...]
+
+    def columns(width, step, side):
+        row, lane = iota((8, width), 0), iota((8, width), 1)
+        pick = jnp.where((row < 6) & (lane == step * row + side), 1.0, 0.0)
+        return lax.dot_general(
+            rest, pick, (((0,), (0,)), ((), ())),
+            precision=lax.Precision.HIGHEST, preferred_element_type=F32,
+        )
+
+    kernel_grad = columns(12, 2, 0)[0:48] + columns(12, 2, 1)[48:96]
+    for offset in range(3):
+        for i in range(4):
+            at = 16 * offset + 4 * i
+            kernel_out[offset, i] = kernel_grad[at : at + 4]
+    gain_out[...] = columns(6, 1, 0)[96:98]
+    for copy in copies:
+        copy.wait()
+
+
+def hand_out(results, rest):
+    vmem = pl.BlockSpec(memory_space=pltpu.VMEM)
+    hbm = pl.BlockSpec(memory_space=pl.ANY)
+    shape = jax.ShapeDtypeStruct
+    return pl.pallas_call(
+        hand_out_kernel,
+        in_specs=[hbm] * 6 + [vmem],
+        out_specs=[hbm] * 6 + [vmem] * 2,
+        out_shape=[shape(array.shape, array.dtype) for array in results]
+        + [shape((3, 4, 4, 12), F32), shape((2, 6), F32)],
+        scratch_shapes=[pltpu.SemaphoreType.DMA((6,))],
+        compiler_params=pltpu.CompilerParams(vmem_limit_bytes=62 * MIB),
+        name="hand_out",
+    )(*results, rest)
+
+
 def shards(half_one, half_two, grad_one, grad_two, norm_gain, attn_weight, mlp_weight, pool_kernel):
-    input_one, input_two, total, input_grad_two, mlp_sums, attn_sums, rest = run_block(
+    *results, rest = run_block(
         half_one, half_two, grad_one, grad_two, norm_gain, attn_weight, mlp_weight, pool_kernel
+    )
+    (input_one, input_two, total, input_grad_two, mlp_sums, attn_sums, kernel_grad, gain_grad) = (
+        hand_out(results, rest)
     )
     mlp_grad = mlp_sums.transpose(1, 2, 0)
     attn_grad = attn_sums.transpose(1, 2, 0)
-    kernel_grad = rest[0:6, 0:96].reshape(6, 2, 48).transpose(2, 0, 1).reshape(3, 4, 4, 12)
-    gain_grad = rest[0:6, 96:98].T
     return (input_one, input_two, total, input_grad_two, attn_grad, mlp_grad, kernel_grad, gain_grad)
 
 

time: 127 us -> 164 us (1.29)
  Pallas kernels: 113 us -> 163 us
  local copies, waits for them, and re-layouts: 13 us -> 0 us
    pallas_call x0 -> x1, Pallas kernels: none -> 50.8 us  [hand_out(): pl.pallas_call(hand_out_kernel, in_specs=[hbm] * 6 + [vmem], out_specs=[h...]
    unnamed x8 -> x0, local copies, waits for them, and re-layouts: 11.4 us -> none
where the time goes in v3:
time: 164 us
  Pallas kernels  163 us (99%)
    pallas_call x1, Pallas kernels, run_block(): pl.pallas_call(block_kernel, in_specs=[hbm, hbm, hbm, hbm, vmem, hbm, hbm...  112 us
    pallas_call x1, Pallas kernels, hand_out(): pl.pallas_call(hand_out_kernel, in_specs=[hbm] * 6 + [vmem], out_specs=[h...  50.8 us

profile of v3, /device:TPU:1, one launch (start us, length us, event | category | flops | bytes accessed | tf_op | source)
XLA Modules:
  0.0 163.6 jit_solution(16365637412544461651)
XLA Ops:
  0.6 112.0 %reversible_block.1 = (bf16[1,1,14,14,768]{4,3,2,1,0:T(8,128)(2,1)}, bf16[1,1,14,14,768]{4,3,2,1,0:T(8,128)(2,1)}, bf16[1,1,14,14,768]{4,3,2,1,0:T(8,128)(2,1)},...) custom-call(bf16[1,1,14,14,768]{4,3,2,1,0:T(8,128)(2,1)} %one_hbm.1, ...), custom_call_target="tpu_custom_call" | custom-call | tf_op jit(solution)/shard_map/reversible_block/pallas_call | solution.py:732
  112.6 50.8 %hand_out.1 = (bf16[1,1,14,14,768]{4,3,2,1,0:T(8,128)(2,1)}, bf16[1,1,14,14,768]{4,3,2,1,0:T(8,128)(2,1)}, bf16[1,1,14,14,768]{4,3,2,1,0:T(8,128)(2,1)}, bf16[1,...) custom-call(bf16[1,1,14,14,768]{4,3,2,1,0:T(8,128)(2,1)} %get-tuple-, ...), custom_call_target="tpu_custom_call" | custom-call | tf_op jit(solution)/shard_map/hand_out/pallas_call | solution.py:780

commit v4 on v3

--- a/solution.py
+++ b/solution.py
@@ -259,11 +259,12 @@
             self.store(part, (first - self.parts[part][0]) // 512, total)
 
 
-MLP_PARTS = tuple((p * 2048, 2048) for p in range(3))
+MLP_PARTS = ((3072, 1536), (0, 3072), (4608, 1536))
 FIRST_PARTS = tuple((p * 512, 512) for p in range(3))
 LAST_PARTS = ((0, 512), (512, 512), (1024, 640))
 MLP_COLS, FIRST_COLS, LAST_COLS = 6144, 1536, 1664
-CHUNK_ORDER = (0, 1, 4, 5, 2, 3)
+PIECES = ((1, 0, 0, 512), (1, 1, 0, 512), (1, 2, 0, 512), (0, 3, 0, 512), (2, 4, 0, 512),
+          (2, 5, 256, 256), (0, 5, 0, 256))
 N_COPIES = 6 + 3 * 9 + 2 * 30 + 6 + 12 + 18 + 6
 
 
@@ -296,7 +297,7 @@
     mlp_own, mlp_land = take(1)[0], take(6)
     first_land, last_land = take(6), take(6)
     attn, orders, pool, pad = take(4)
-    normed, cot, branch, d_normed = take(4)
+    normed, cot, branch = take(3)
     normed_two, query, keyval, d_att, total, lefts = take(6)
     parts, from_pair, from_edge = take(3)
     keys, values, d_keys, d_values = take(4)
@@ -319,7 +320,7 @@
     one_copy, cot_two_copy, two_copy, cot_one_copy, pool_copy, attn_copy = fetches
 
     def weight_copies(k):
-        rows = pl.ds(CHUNK_ORDER[k] * CHUNK, CHUNK)
+        rows = pl.ds(k % STEPS * CHUNK, CHUNK)
         return [
             pltpu.make_async_copy(mlp_hbm.at[0, rows], up_buf.at[k % 2], weight_sem.at[0, k % 2]),
             pltpu.make_async_copy(mlp_hbm.at[1, rows], down_buf.at[k % 2], weight_sem.at[1, k % 2]),
@@ -348,8 +349,13 @@
         writes.append(copy)
 
     def store_mlp(part, block, values):
-        at = pl.ds((2 * part + block // 2) * CHUNK, CHUNK)
-        mlp_sums[:, block % 2, at] = values[0:6]
+        _, chunk, begin, units = [piece for piece in PIECES if piece[0] == part][block // 2]
+        at = pl.ds(chunk * CHUNK + begin, units)
+        if units == CHUNK:
+            mlp_sums[:, block % 2, at] = values[0:6]
+        else:
+            for side in range(2):
+                mlp_sums[:, side, at] = values[0:6, side * units : (side + 1) * units]
 
     def store_first(part, block, values):
         at = pl.ds(part * 256, 256)
@@ -369,21 +375,27 @@
     first = Reduction(links, place, FIRST_PARTS, stage, own_base, 0, first_land, store_first)
     last = Reduction(links, place, LAST_PARTS, stage, own_base, FIRST_COLS, last_land, store_last)
 
+    def kept(chunk):
+        if chunk == STEPS - 1:
+            return attended.at[:, pl.ds(0, CHUNK)], d_query.at[:, pl.ds(0, CHUNK)]
+        at = chunk * 2 * CHUNK
+        rows = pl.ds(0, ROWS)
+        return mlp_own.at[rows, pl.ds(at, CHUNK)], mlp_own.at[rows, pl.ds(at + CHUNK, CHUNK)]
+
+    def next_weights(k):
+        if k + 2 < 2 * STEPS:
+            for copy in weight_copies(k + 2):
+                copy.start()
+
+    for part in (1, 0, 2):
+        orders[part] = permutation(part)
     one_copy.wait()
     unit, scale = norm_stats(load_padded(one_in, pad).astype(F32))
     normed[...] = (unit * gain_ref[0:1, :]).astype(BF16)
-    cot_two_copy.wait()
-    cot[...] = load_padded(cot_two_in, pad)
-    for k, chunk in enumerate(CHUNK_ORDER):
-        part = chunk // 2
-        if chunk % 2 == 0:
-            orders[part] = permutation(part)
-            lefts[0] = dot_nt(orders[part], normed[...]).astype(BF16)
-            lefts[1] = dot_nt(orders[part], cot[...]).astype(BF16)
+    for k in range(STEPS):
         for copy in weight_copies(k):
             copy.wait()
-        up, down = up_buf[k % 2], down_buf[k % 2]
-        hidden = dot_nt(normed[...], up)
+        hidden = dot_nt(normed[...], up_buf[k % 2])
         inner = 0.7978845608028654 * (hidden + 0.044715 * hidden * hidden * hidden)
         tanh = jnp.tanh(inner)
         half_sum = 0.5 * (1.0 + tanh)
@@ -391,41 +403,54 @@
         slope = half_sum + 0.5 * hidden * (1.0 - tanh * tanh) * (
             0.7978845608028654 * (1.0 + 3.0 * 0.044715 * hidden * hidden)
         )
-        d_hidden = (slope * dot_nt(cot[...], down)).astype(BF16)
+        active_at, slope_at = kept(k)
+        active_at[...] = active
+        slope_at[...] = slope.astype(BF16)
         if k == 0:
-            branch[...] = dot(active, down)
-            d_normed[...] = dot(d_hidden, up)
+            branch[...] = dot(active, down_buf[k % 2])
         else:
-            branch[...] += dot(active, down)
-            d_normed[...] += dot(d_hidden, up)
-        if k + 2 < STEPS:
-            for copy in weight_copies(k + 2):
-                copy.start()
-        at = (chunk % 2) * HALF
-        cols = part * 2 * CHUNK
-        for side, values_in in enumerate((d_hidden, active)):
-            rows = pl.ds(other_base, HALF)
-            stage[pl.ds(at, HALF), pl.ds(cols + side * CHUNK, CHUNK)] = dot(
-                lefts[side, rows], values_in
-            ).astype(BF16)
-        if k == 0:
-            pl.semaphore_wait(barrier, len(partners))
-        mlp.copies.setdefault((0, part), []).append(
-            links.start(
-                stage.at[pl.ds(at, HALF), pl.ds(cols, 2 * CHUNK)],
-                mlp.in0.at[:, pl.ds(chunk * 2 * CHUNK, 2 * CHUNK)],
-                place.other_core(),
+            branch[...] += dot(active, down_buf[k % 2])
+        next_weights(k)
+
+    def back(chunk):
+        k = STEPS + chunk
+        for copy in weight_copies(k):
+            copy.wait()
+        up, down = up_buf[k % 2], down_buf[k % 2]
+        active_at, slope_at = kept(chunk)
+        active = active_at[...]
+        d_hidden = (slope_at[...].astype(F32) * dot_nt(cot[...], down)).astype(BF16)
+        if chunk == 0:
+            branch[...] = dot(d_hidden, up)
+        else:
+            branch[...] += dot(d_hidden, up)
+        next_weights(k)
+        for number, (part, at_chunk, begin, units) in enumerate(PIECES):
+            if at_chunk != chunk:
+                continue
+            if number == 0 or PIECES[number - 1][0] != part:
+                lefts[0] = dot_nt(orders[part], normed[...]).astype(BF16)
+                lefts[1] = dot_nt(orders[part], cot[...]).astype(BF16)
+            row = 0 if number in (0, 2, 4) else HALF
+            col = 2560 if number == 6 else (number // 2) * 2 * CHUNK
+            first_col = MLP_PARTS[part][0]
+            for piece in PIECES[:number]:
+                first_col += 2 * piece[3] if piece[0] == part else 0
+            for side, values_in in enumerate((d_hidden, active)):
+                values_in = values_in[:, begin : begin + units]
+                stage[pl.ds(row, HALF), pl.ds(col + side * units, units)] = dot(
+                    lefts[side, pl.ds(other_base, HALF)], values_in
+                ).astype(BF16)
+                mlp_own[:, pl.ds(first_col + side * units, units)] = dot(
+                    lefts[side, pl.ds(own_base, HALF)], values_in
+                ).astype(BF16)
+            mlp.copies.setdefault((0, part), []).append(
+                links.start(
+                    stage.at[pl.ds(row, HALF), pl.ds(col, 2 * units)],
+                    mlp.in0.at[:, pl.ds(first_col, 2 * units)],
+                    place.other_core(),
+                )
             )
-        )
-        for side, values_in in enumerate((d_hidden, active)):
-            rows = pl.ds(own_base, HALF)
-            mlp_own[:, pl.ds(chunk * 2 * CHUNK + side * CHUNK, CHUNK)] = dot(
-                lefts[side, rows], values_in
-            ).astype(BF16)
-        if k == 2:
-            mlp.send1(0)
-        if k == 4:
-            mlp.send1(2)
 
     two_copy.wait()
     restored = (load_padded(two_in, pad).astype(F32) - branch[...]).astype(BF16)
@@ -445,6 +470,7 @@
         parts[2 - offset] = gather_rows(blocks, weighted).astype(BF16)
 
     mine = pl.ds(1 - low, 2)
+    pl.semaphore_wait(barrier, len(partners))
     pair_copy = links.start(parts.at[mine], from_pair, place.pair(0, 1 - low))
     edge_base = links.used
     for side in range(2):
@@ -453,16 +479,10 @@
             (place.clip, (place.tm - low + 4 * low - 2 + 32) % 32 + side),
             shift=1 - low if side == 0 else -low, slots=1,
         )
-    mlp.send1(1)
     query[...] = dot(normed_two[...], attn[0]).astype(BF16)
-    back = d_normed[...]
-    unit, scale = norm_stats(load_padded(one_in, pad).astype(F32))
-    d_gain_one = jnp.sum(back * unit, axis=0, keepdims=True)
-    d_first = norm_back(unit, scale, gain_ref[0:1, :], back)
-    cot_one_copy.wait()
-    total[...] = (load_padded(cot_one_in, pad).astype(F32) + d_first).astype(BF16)
-    store_grid(cot_one_in, total[...])
-    write(cot_one_in, total_out)
+    cot_two_copy.wait()
+    cot[...] = load_padded(cot_two_in, pad)
+    back(0)
     pair_copy.wait_recv()
     for slot in range(2):
         links.arrival(from_edge.at[slot], edge_base + slot)
@@ -478,17 +498,31 @@
     for hop in (2, 1, 3):
         copies.append(links.start(keys.at[x, z], keys.at[x, z], place.along(2, hop)[0]))
         copies.append(links.start(values.at[x, z], values.at[x, z], place.along(0, hop)[0]))
-    d_att[...] = dot_nt(total[...], attn[3]).astype(BF16)
+    back(1)
     for copy in copies:
         copy.wait_recv()
     copies = []
     for hop in (2, 1, 3):
         copies.append(links.start(keys.at[x], keys.at[x], place.along(0, hop)[0]))
         copies.append(links.start(values.at[:, z], values.at[:, z], place.along(2, hop)[0]))
+    for chunk in range(2, STEPS):
+        back(chunk)
+        if chunk == 3:
+            mlp.send1(1)
+    unit, scale = norm_stats(load_padded(one_in, pad).astype(F32))
+    d_gain_one = jnp.sum(branch[...] * unit, axis=0, keepdims=True)
+    d_first = norm_back(unit, scale, gain_ref[0:1, :], branch[...])
+    cot_one_copy.wait()
+    total[...] = (load_padded(cot_one_in, pad).astype(F32) + d_first).astype(BF16)
+    store_grid(cot_one_in, total[...])
+    write(cot_one_in, total_out)
+    d_att[...] = dot_nt(total[...], attn[3]).astype(BF16)
     for part in range(3):
         lefts[part] = dot_nt(orders[part], total[...]).astype(BF16)
     for copy in copies:
         copy.wait_recv()
+    mlp.send1(0)
+    mlp.send1(2)
 
     def heads(pair, carry):
         lanes = pl.ds(pl.multiple_of(pair * 128, 128), 128)
@@ -539,8 +573,6 @@
                 links.start(d_values.at[:, at, :, lanes], z_values.at[hop - 1, :, :, lanes], device)
             )
 
-    for part in (0, 2):
-        mlp.send2(part)
     for part in range(3):
         for copy in mlp.copies[0, part]:
             links.sent(copy)
@@ -555,7 +587,7 @@
             lefts[part], attended[:, inside]
         ).astype(BF16)
         first.send0(part)
-    d_normed[...] = dot_nt(d_query[...], attn[0])
+    branch[...] = dot_nt(d_query[...], attn[0])
 
     for copy in copies:
         copy.wait_recv()
@@ -572,7 +604,8 @@
         copies.append(links.start(key_sum.at[at], z_keys.at[hop - 1], device))
         device, at = place.along(0, hop)
         copies.append(links.start(value_sum.at[at], x_values.at[hop - 1], device))
-    mlp.send2(1)
+    mlp.send2(0)
+    mlp.send2(2)
     for copy in copies:
         copy.wait_recv()
     sum_k = key_sum[z].astype(F32)
@@ -593,6 +626,7 @@
         )
     for part in range(3):
         first.send1(part)
+    mlp.send2(1)
     pair_copy.wait_recv()
     for slot in range(2):
         links.arrival(edge_land.at[slot], edge_base + slot)
@@ -631,7 +665,7 @@
         last_part(part)
         last.send0(part)
     last_part(2)
-    d_normed_two = d_normed[...] + dot_nt(d_key_proj, attn[1]) + dot_nt(d_value_proj, attn[2])
+    d_normed_two = branch[...] + dot_nt(d_key_proj, attn[1]) + dot_nt(d_value_proj, attn[2])
     d_second = norm_back(unit_two, scale_two, gain_ref[1:2, :], d_normed_two)
     extra_gain[...] = jnp.zeros(extra_gain.shape, F32)
     extra_gain[96:97, :] = d_gain_one
@@ -699,7 +733,6 @@
         pltpu.VMEM((14, 16, D), BF16),
         pltpu.VMEM((ROWS, D), BF16),
         pltpu.VMEM((ROWS, D), BF16),
-        pltpu.VMEM((ROWS, D), F32),
         pltpu.VMEM((ROWS, D), F32),
         pltpu.VMEM((ROWS, D), BF16),
         pltpu.VMEM((ROWS, D), BF16),
@@ -746,12 +779,20 @@
 
 
 def hand_out_kernel(*refs):
-    taken, rest_ref, given, kernel_out, gain_out, sem = refs[0:6], refs[6], refs[7:13], *refs[13:]
+    taken, rest_ref, given, kernel_out, gain_out = refs[0:6], refs[6], refs[7:13], *refs[13:15]
+    held, in_sem, out_sem = refs[15:21], *refs[21:]
+    loads = [
+        pltpu.make_async_copy(source, target, in_sem.at[k])
+        for k, (source, target) in enumerate(zip(taken, held))
+    ]
     copies = [
-        pltpu.make_async_copy(source, target, sem.at[k])
-        for k, (source, target) in enumerate(zip(taken, given))
+        pltpu.make_async_copy(source, target, out_sem.at[k])
+        for k, (source, target) in enumerate(zip(held, given))
     ]
-    for copy in copies:
+    for load in loads:
+        load.start()
+    for load, copy in zip(loads, copies):
+        load.wait()
         copy.start()
     rest = rest_ref[...]
 
@@ -783,7 +824,8 @@
         out_specs=[hbm] * 6 + [vmem] * 2,
         out_shape=[shape(array.shape, array.dtype) for array in results]
         + [shape((3, 4, 4, 12), F32), shape((2, 6), F32)],
-        scratch_shapes=[pltpu.SemaphoreType.DMA((6,))],
+        scratch_shapes=[pltpu.VMEM(array.shape, array.dtype) for array in results]
+        + [pltpu.SemaphoreType.DMA((6,)), pltpu.SemaphoreType.DMA((6,))],
         compiler_params=pltpu.CompilerParams(vmem_limit_bytes=62 * MIB),
         name="hand_out",
     )(*results, rest)

time: 164 us -> 109 us (0.66)
  Pallas kernels: 163 us -> 107 us
    pallas_call x1, Pallas kernels: 50.8 us -> 3.5 us  [hand_out(): pl.pallas_call(hand_out_kernel, in_specs=[hbm] * 6 + [vmem], out_specs=[h...]
    pallas_call x1, Pallas kernels: 112 us -> 103 us  [run_block(): pl.pallas_call(block_kernel, in_specs=[hbm, hbm, hbm, hbm, vmem, hbm, hbm...]
where the time goes in v4:
time: 109 us; the launch traced here: 108 us
  Pallas kernels  107 us (98%)
    pallas_call x1, Pallas kernels, run_block(): pl.pallas_call(block_kernel, in_specs=[hbm, hbm, hbm, hbm, vmem, hbm, hbm...  103 us
    pallas_call x1, Pallas kernels, hand_out(): pl.pallas_call(hand_out_kernel, in_specs=[hbm] * 6 + [vmem], out_specs=[h...  3.5 us

profile of v4, /device:TPU:1, one launch (start us, length us, event | category | flops | bytes accessed | tf_op | source)
XLA Modules:
  0.0 107.7 jit_solution(13805033490881838225)
XLA Ops:
  0.6 103.4 %reversible_block.1 = (bf16[1,1,14,14,768]{4,3,2,1,0:T(8,128)(2,1)}, bf16[1,1,14,14,768]{4,3,2,1,0:T(8,128)(2,1)}, bf16[1,1,14,14,768]{4,3,2,1,0:T(8,128)(2,1)},...) custom-call(bf16[1,1,14,14,768]{4,3,2,1,0:T(8,128)(2,1)} %one_hbm.1, ...), custom_call_target="tpu_custom_call" | custom-call | tf_op jit(solution)/shard_map/reversible_block/pallas_call | solution.py:765
  104.0 3.5 %hand_out.1 = (bf16[1,1,14,14,768]{4,3,2,1,0:T(8,128)(2,1)}, bf16[1,1,14,14,768]{4,3,2,1,0:T(8,128)(2,1)}, bf16[1,1,14,14,768]{4,3,2,1,0:T(8,128)(2,1)}, bf16[1,...) custom-call(bf16[1,1,14,14,768]{4,3,2,1,0:T(8,128)(2,1)} %get-tuple-, ...), custom_call_target="tpu_custom_call" | custom-call | tf_op jit(solution)/shard_map/hand_out/pallas_call | solution.py:821

commit v5 on v4

--- a/solution.py
+++ b/solution.py
@@ -36,18 +36,18 @@
     return lax.broadcasted_iota(jnp.int32, shape, dim)
 
 
-def source_column(rows, part):
+def source_column(rows, axes):
     owner_at = (rows * 43691) >> 18
     inner = rows - owner_at * 6
     core = owner_at >> 6
     digits = ((owner_at >> 4) & 3, (owner_at >> 2) & 3, owner_at & 3)
-    x, y, z = (digits[(axis - part) % 3] for axis in range(3))
+    x, y, z = (digits[axes.index(axis)] for axis in range(3))
     owner = (y >> 1) * 64 + core * 32 + x * 8 + z * 2 + (y & 1)
     return owner * 6 + inner
 
 
-def permutation(part):
-    source = source_column(iota((D, 128), 0), part)
+def permutation(axes):
+    source = source_column(iota((D, 128), 0), axes)
     lanes = iota((D, 128), 1)
     pieces = [
         jnp.where(source == lanes + 128 * k, 1.0, 0.0).astype(BF16) for k in range(D // 128)
@@ -103,9 +103,7 @@
 
 
 def gather_rows(one_hot, values):
-    high = values.astype(BF16)
-    low = (values - high.astype(F32)).astype(BF16)
-    return dot_tn(one_hot, high) + dot_tn(one_hot, low)
+    return dot_tn(one_hot, values.astype(BF16))
 
 
 class Links:
@@ -160,8 +158,9 @@
 
 
 class Reduction:
-    def __init__(self, links, place, parts, held, base, offset, landed, store):
+    def __init__(self, links, place, parts, orders, held, base, offset, landed, store):
         self.links, self.place, self.parts = links, place, parts
+        self.axes = [ORDERS[order] for order in orders]
         self.held, self.base, self.offset = held, base, offset
         self.in0, self.in1, self.sum1, self.in2, self.sum2, self.in3 = landed
         self.store = store
@@ -191,7 +190,7 @@
             copy.wait_recv()
 
     def spread(self, stage, part, source, base, offset, rows, target):
-        axis = (part + stage - 1) % 3
+        axis = self.axes[part][stage - 1]
         cols = self.columns(part)
         source_cols = self.columns(part, offset)
         self.copies[stage, part] = []
@@ -221,7 +220,7 @@
 
     def send2(self, part):
         self.arrive(1, part)
-        mine = self.place.at[part % 3]
+        mine = self.place.at[self.axes[part][0]]
         rows = pl.ds(pl.multiple_of(self.base + mine * 96, 96), 96)
         place_row, place_col = iota((128, 96), 0), iota((128, 96), 1)
         owner = place_row >> 3
@@ -237,7 +236,7 @@
 
     def send3(self, part):
         self.arrive(2, part)
-        mine = self.place.at[(part + 1) % 3]
+        mine = self.place.at[self.axes[part][1]]
         rows = pl.ds(pl.multiple_of(mine * 32, 32), 32)
         for first, count in self.blocks(part):
             cols = pl.ds(first, count)
@@ -249,7 +248,7 @@
 
     def finish(self, part):
         self.arrive(3, part)
-        mine = self.place.at[(part + 2) % 3]
+        mine = self.place.at[self.axes[part][2]]
         rows = pl.ds(pl.multiple_of(mine * 8, 8), 8)
         for first, count in self.blocks(part):
             cols = pl.ds(first, count)
@@ -259,13 +258,13 @@
             self.store(part, (first - self.parts[part][0]) // 512, total)
 
 
-MLP_PARTS = ((3072, 1536), (0, 3072), (4608, 1536))
+ORDERS = ((0, 1, 2), (1, 2, 0), (2, 0, 1), (1, 0, 2))
+MLP_ORDERS = (1, 1, 3, 3, 0, 2)
+MLP_PARTS = tuple((k * 1024, 1024) for k in range(STEPS))
 FIRST_PARTS = tuple((p * 512, 512) for p in range(3))
 LAST_PARTS = ((0, 512), (512, 512), (1024, 640))
 MLP_COLS, FIRST_COLS, LAST_COLS = 6144, 1536, 1664
-PIECES = ((1, 0, 0, 512), (1, 1, 0, 512), (1, 2, 0, 512), (0, 3, 0, 512), (2, 4, 0, 512),
-          (2, 5, 256, 256), (0, 5, 0, 256))
-N_COPIES = 6 + 3 * 9 + 2 * 30 + 6 + 12 + 18 + 6
+N_COPIES = 6 * 10 + 2 * 30 + 3 + 12 + 24 + 3
 
 
 def landing(cols):
@@ -322,17 +321,14 @@
     def weight_copies(k):
         rows = pl.ds(k % STEPS * CHUNK, CHUNK)
         return [
-            pltpu.make_async_copy(mlp_hbm.at[0, rows], up_buf.at[k % 2], weight_sem.at[0, k % 2]),
-            pltpu.make_async_copy(mlp_hbm.at[1, rows], down_buf.at[k % 2], weight_sem.at[1, k % 2]),
+            pltpu.make_async_copy(mlp_hbm.at[0, rows], up_buf.at[k % 3], weight_sem.at[0, k % 3]),
+            pltpu.make_async_copy(mlp_hbm.at[1, rows], down_buf.at[k % 3], weight_sem.at[1, k % 3]),
         ]
 
     one_copy.start()
-    cot_two_copy.start()
-    for k in range(2):
+    for k in range(3):
         for copy in weight_copies(k):
             copy.start()
-    for copy in fetches[2:]:
-        copy.start()
 
     barrier = pltpu.get_barrier_semaphore()
     partners = [place.other_core()]
@@ -349,13 +345,7 @@
         writes.append(copy)
 
     def store_mlp(part, block, values):
-        _, chunk, begin, units = [piece for piece in PIECES if piece[0] == part][block // 2]
-        at = pl.ds(chunk * CHUNK + begin, units)
-        if units == CHUNK:
-            mlp_sums[:, block % 2, at] = values[0:6]
-        else:
-            for side in range(2):
-                mlp_sums[:, side, at] = values[0:6, side * units : (side + 1) * units]
+        mlp_sums[:, block, pl.ds(part * CHUNK, CHUNK)] = values[0:6]
 
     def store_first(part, block, values):
         at = pl.ds(part * 256, 256)
@@ -371,31 +361,29 @@
 
     own_base = pl.multiple_of(place.core * HALF, HALF)
     other_base = pl.multiple_of((1 - place.core) * HALF, HALF)
-    mlp = Reduction(links, place, MLP_PARTS, mlp_own, 0, 0, mlp_land, store_mlp)
-    first = Reduction(links, place, FIRST_PARTS, stage, own_base, 0, first_land, store_first)
-    last = Reduction(links, place, LAST_PARTS, stage, own_base, FIRST_COLS, last_land, store_last)
+    mlp = Reduction(links, place, MLP_PARTS, MLP_ORDERS, mlp_own, 0, 0, mlp_land, store_mlp)
+    first = Reduction(links, place, FIRST_PARTS, (0, 1, 2), stage, own_base, 0, first_land, store_first)
+    last = Reduction(links, place, LAST_PARTS, (0, 1, 2), stage, own_base, FIRST_COLS, last_land, store_last)
 
     def kept(chunk):
-        if chunk == STEPS - 1:
-            return attended.at[:, pl.ds(0, CHUNK)], d_query.at[:, pl.ds(0, CHUNK)]
         at = chunk * 2 * CHUNK
         rows = pl.ds(0, ROWS)
         return mlp_own.at[rows, pl.ds(at, CHUNK)], mlp_own.at[rows, pl.ds(at + CHUNK, CHUNK)]
 
     def next_weights(k):
-        if k + 2 < 2 * STEPS:
-            for copy in weight_copies(k + 2):
+        if k + 3 < 2 * STEPS:
+            for copy in weight_copies(k + 3):
                 copy.start()
 
-    for part in (1, 0, 2):
-        orders[part] = permutation(part)
+    for k, axes in enumerate(ORDERS):
+        orders[k] = permutation(axes)
     one_copy.wait()
     unit, scale = norm_stats(load_padded(one_in, pad).astype(F32))
     normed[...] = (unit * gain_ref[0:1, :]).astype(BF16)
     for k in range(STEPS):
         for copy in weight_copies(k):
             copy.wait()
-        hidden = dot_nt(normed[...], up_buf[k % 2])
+        hidden = dot_nt(normed[...], up_buf[k % 3])
         inner = 0.7978845608028654 * (hidden + 0.044715 * hidden * hidden * hidden)
         tanh = jnp.tanh(inner)
         half_sum = 0.5 * (1.0 + tanh)
@@ -407,16 +395,22 @@
         active_at[...] = active
         slope_at[...] = slope.astype(BF16)
         if k == 0:
-            branch[...] = dot(active, down_buf[k % 2])
+            branch[...] = dot(active, down_buf[k % 3])
         else:
-            branch[...] += dot(active, down_buf[k % 2])
+            branch[...] += dot(active, down_buf[k % 3])
         next_weights(k)
+        if k == 2:
+            two_copy.start()
+            pool_copy.start()
+            attn_copy.start()
+            cot_two_copy.start()
+            cot_one_copy.start()
 
     def back(chunk):
         k = STEPS + chunk
         for copy in weight_copies(k):
             copy.wait()
-        up, down = up_buf[k % 2], down_buf[k % 2]
+        up, down = up_buf[k % 3], down_buf[k % 3]
         active_at, slope_at = kept(chunk)
         active = active_at[...]
         d_hidden = (slope_at[...].astype(F32) * dot_nt(cot[...], down)).astype(BF16)
@@ -425,32 +419,28 @@
         else:
             branch[...] += dot(d_hidden, up)
         next_weights(k)
-        for number, (part, at_chunk, begin, units) in enumerate(PIECES):
-            if at_chunk != chunk:
-                continue
-            if number == 0 or PIECES[number - 1][0] != part:
-                lefts[0] = dot_nt(orders[part], normed[...]).astype(BF16)
-                lefts[1] = dot_nt(orders[part], cot[...]).astype(BF16)
-            row = 0 if number in (0, 2, 4) else HALF
-            col = 2560 if number == 6 else (number // 2) * 2 * CHUNK
-            first_col = MLP_PARTS[part][0]
-            for piece in PIECES[:number]:
-                first_col += 2 * piece[3] if piece[0] == part else 0
-            for side, values_in in enumerate((d_hidden, active)):
-                values_in = values_in[:, begin : begin + units]
-                stage[pl.ds(row, HALF), pl.ds(col + side * units, units)] = dot(
-                    lefts[side, pl.ds(other_base, HALF)], values_in
-                ).astype(BF16)
-                mlp_own[:, pl.ds(first_col + side * units, units)] = dot(
-                    lefts[side, pl.ds(own_base, HALF)], values_in
-                ).astype(BF16)
-            mlp.copies.setdefault((0, part), []).append(
-                links.start(
-                    stage.at[pl.ds(row, HALF), pl.ds(col, 2 * units)],
-                    mlp.in0.at[:, pl.ds(first_col, 2 * units)],
-                    place.other_core(),
-                )
+        order = MLP_ORDERS[chunk]
+        if chunk == 0 or MLP_ORDERS[chunk - 1] != order:
+            lefts[0] = dot_nt(orders[order], normed[...]).astype(BF16)
+            lefts[1] = dot_nt(orders[order], cot[...]).astype(BF16)
+        row = chunk % 2 * HALF
+        col = chunk // 2 * 2 * CHUNK
+        first_col = chunk * 2 * CHUNK
+        for side, values_in in enumerate((d_hidden, active)):
+            stage[pl.ds(row, HALF), pl.ds(col + side * CHUNK, CHUNK)] = dot(
+                lefts[side, pl.ds(other_base, HALF)], values_in
+            ).astype(BF16)
+        mlp.copies[0, chunk] = [
+            links.start(
+                stage.at[pl.ds(row, HALF), pl.ds(col, 2 * CHUNK)],
+                mlp.in0.at[:, pl.ds(first_col, 2 * CHUNK)],
+                place.other_core(),
             )
+        ]
+        for side, values_in in enumerate((d_hidden, active)):
+            mlp_own[:, pl.ds(first_col + side * CHUNK, CHUNK)] = dot(
+                lefts[side, pl.ds(own_base, HALF)], values_in
+            ).astype(BF16)
 
     two_copy.wait()
     restored = (load_padded(two_in, pad).astype(F32) - branch[...]).astype(BF16)
@@ -506,9 +496,8 @@
         copies.append(links.start(keys.at[x], keys.at[x], place.along(0, hop)[0]))
         copies.append(links.start(values.at[:, z], values.at[:, z], place.along(2, hop)[0]))
     for chunk in range(2, STEPS):
+        mlp.send1(chunk - 2)
         back(chunk)
-        if chunk == 3:
-            mlp.send1(1)
     unit, scale = norm_stats(load_padded(one_in, pad).astype(F32))
     d_gain_one = jnp.sum(branch[...] * unit, axis=0, keepdims=True)
     d_first = norm_back(unit, scale, gain_ref[0:1, :], branch[...])
@@ -521,16 +510,16 @@
         lefts[part] = dot_nt(orders[part], total[...]).astype(BF16)
     for copy in copies:
         copy.wait_recv()
-    mlp.send1(0)
-    mlp.send1(2)
-
-    def heads(pair, carry):
-        lanes = pl.ds(pl.multiple_of(pair * 128, 128), 128)
-        query_pair = query[:, lanes]
+    mlp.send1(4)
+    mlp.send1(5)
+
+    def heads(pair):
+        lanes = pl.ds(pair * 128, 128)
+        query_pair = query[:, lanes] * jnp.asarray(0.125, BF16)
         d_att_pair = d_att[:, lanes]
         key = keys[:, :, :, lanes].reshape(512, 128)
         value = values[:, :, :, lanes].reshape(512, 128)
-        att = d_q = d_k = d_v = None
+        queries, d_atts, keys_h, values_h, probs_h, d_scores_h = [], [], [], [], [], []
         for side in range(2):
 
             def only(array):
@@ -538,31 +527,34 @@
                 keep = lane < 64 if side == 0 else lane >= 64
                 return jnp.where(keep, array, jnp.zeros_like(array))
 
-            query_h, d_att_h = only(query_pair), only(d_att_pair)
-            weights = jnp.exp(dot_nt(query_h, key) * 0.125)
+            queries.append(only(query_pair))
+            d_atts.append(only(d_att_pair))
+            keys_h.append(only(key))
+            values_h.append(only(value))
+            weights = jnp.exp(dot_nt(queries[side], key))
             probs = weights * (1.0 / jnp.sum(weights, axis=-1, keepdims=True))
-            probs_b = probs.astype(BF16)
-            d_probs = dot_nt(d_att_h, value)
-            product = probs * d_probs
-            d_scores = (product - probs * jnp.sum(product, axis=-1, keepdims=True)).astype(BF16)
-            terms = (
-                dot(probs_b, only(value)), dot(d_scores, only(key)),
-                dot_tn(d_scores, query_h), dot_tn(probs_b, d_att_h),
-            )
-            if side == 0:
-                att, d_q, d_k, d_v = terms
-            else:
-                att, d_q, d_k, d_v = (a + b for a, b in zip((att, d_q, d_k, d_v), terms))
+            product = probs * dot_nt(d_atts[side], value)
+            d_scores = product - probs * jnp.sum(product, axis=-1, keepdims=True)
+            probs_h.append(probs.astype(BF16))
+            d_scores_h.append(d_scores.astype(BF16))
+
+        def joined(pieces, axis):
+            return jnp.concatenate(pieces, axis=axis)
+
+        att = dot(joined(probs_h, 1), joined(values_h, 0))
+        d_q = dot(joined(d_scores_h, 1), joined(keys_h, 0)) * 0.125
+        d_k = dot_tn(joined(d_scores_h, 0), joined(queries, 0))
+        d_v = dot_tn(joined(probs_h, 0), joined(d_atts, 0))
         attended[:, lanes] = att.astype(BF16)
-        d_query[:, lanes] = (d_q * 0.125).astype(BF16)
-        d_keys[:, :, :, lanes] = (d_k * 0.125).astype(BF16).reshape(4, 4, 32, 128)
+        d_query[:, lanes] = d_q.astype(BF16)
+        d_keys[:, :, :, lanes] = d_k.astype(BF16).reshape(4, 4, 32, 128)
         d_values[:, :, :, lanes] = d_v.astype(BF16).reshape(4, 4, 32, 128)
-        return carry
 
     copies = []
-    for group in range(2):
-        lax.fori_loop(3 * group, 3 * group + 3, heads, 0)
-        lanes = pl.ds(group * HALF, HALF)
+    for group in range(3):
+        for pair in range(2 * group, 2 * group + 2):
+            heads(pair)
+        lanes = pl.ds(group * 256, 256)
         for hop in (2, 1, 3):
             device, at = place.along(0, hop)
             copies.append(
@@ -573,7 +565,7 @@
                 links.start(d_values.at[:, at, :, lanes], z_values.at[hop - 1, :, :, lanes], device)
             )
 
-    for part in range(3):
+    for part in range(STEPS):
         for copy in mlp.copies[0, part]:
             links.sent(copy)
     branch_f = dot(attended[...], attn[3])
@@ -604,8 +596,8 @@
         copies.append(links.start(key_sum.at[at], z_keys.at[hop - 1], device))
         device, at = place.along(0, hop)
         copies.append(links.start(value_sum.at[at], x_values.at[hop - 1], device))
-    mlp.send2(0)
-    mlp.send2(2)
+    for part in (0, 1, 4, 5):
+        mlp.send2(part)
     for copy in copies:
         copy.wait_recv()
     sum_k = key_sum[z].astype(F32)
@@ -626,7 +618,8 @@
         )
     for part in range(3):
         first.send1(part)
-    mlp.send2(1)
+    mlp.send2(2)
+    mlp.send2(3)
     pair_copy.wait_recv()
     for slot in range(2):
         links.arrival(edge_land.at[slot], edge_base + slot)
@@ -642,14 +635,12 @@
     cells, blocks = cell_maps()
     keyval_f = keyval[...].astype(F32)
     d_keyval = None
-    extra[...] = jnp.zeros(extra.shape, BF16)
     for offset, source in enumerate((after, here, before)):
         expanded = dot(blocks, source)
         term = spread_kernel(cells, pool[offset]) * expanded
         d_keyval = term if d_keyval is None else d_keyval + term
         d_kernel = gather_rows(cells[:, 0:16], keyval_f * expanded).astype(BF16)
-        extra[0, 16 * offset : 16 * offset + 16, :] = d_kernel
-        extra[1, 48 + 16 * offset : 64 + 16 * offset, :] = d_kernel
+        extra[16 * offset : 16 * offset + 16, :] = d_kernel
     d_keyval = d_keyval.astype(BF16)
     d_key_proj, d_value_proj = d_keyval[:, 0:D], d_keyval[:, D:]
 
@@ -666,40 +657,46 @@
         last.send0(part)
     last_part(2)
     d_normed_two = branch[...] + dot_nt(d_key_proj, attn[1]) + dot_nt(d_value_proj, attn[2])
-    d_second = norm_back(unit_two, scale_two, gain_ref[1:2, :], d_normed_two)
+    row, lane = iota((256, 256), 0), iota((256, 256), 1)
+    parted = jnp.where(row == 2 * (lane & 127) + (lane >> 7), 1.0, 0.0).astype(BF16)
     extra_gain[...] = jnp.zeros(extra_gain.shape, F32)
+    for k in range(6):
+        lanes = pl.ds(k * 128, 128)
+        sides = dot(extra[:, pl.ds(k * 256, 256)], parted)
+        extra_gain[0:48, lanes] = sides[:, 0:128]
+        extra_gain[48:96, lanes] = sides[:, 128:256]
     extra_gain[96:97, :] = d_gain_one
     extra_gain[97:98, :] = jnp.sum(d_normed_two * unit_two, axis=0, keepdims=True)
-    source = source_column(iota((D, 128), 0), 2)
-    lanes = iota((D, 128), 1)
     block = dot_nt(orders[2], extra_gain[...].astype(BF16))
-    for k in range(KV // 128):
-        for side in range(2):
-            pick = jnp.where(2 * source + side == lanes + 128 * k, 1.0, 0.0).astype(BF16)
-            block = block + dot_nt(pick, extra[side, :, k * 128 : (k + 1) * 128])
     stage[:, pl.ds(FIRST_COLS + 1536, 128)] = block.astype(BF16)
     last.send0(2)
+    last.send1(0)
+    last.send1(1)
+    d_second = norm_back(unit_two, scale_two, gain_ref[1:2, :], d_normed_two)
     result = load_padded(cot_two_in, pad).astype(F32) + d_second
     store_grid(cot_two_in, result.astype(BF16))
     write(cot_two_in, grad_two_out)
+    last.send1(2)
 
     for part in range(3):
         first.send2(part)
-    for part in range(3):
-        last.send1(part)
-    for part in range(3):
+    for part in (0, 1, 4, 5):
         mlp.send3(part)
-    for part in range(3):
-        first.send3(part)
     for part in range(3):
         last.send2(part)
     for part in range(3):
+        first.send3(part)
+    mlp.send3(2)
+    mlp.send3(3)
+    for part in (0, 1, 4, 5):
         mlp.finish(part)
-    write(mlp_sums, mlp_out)
     for part in range(3):
         last.send3(part)
     for part in range(3):
         first.finish(part)
+    mlp.finish(2)
+    mlp.finish(3)
+    write(mlp_sums, mlp_out)
     for part in range(3):
         last.finish(part)
     write(attn_sums, attn_out)
@@ -718,17 +715,17 @@
         pltpu.SemaphoreType.DMA((N_COPIES,)),
         pltpu.SemaphoreType.DMA((N_COPIES,)),
         pltpu.SemaphoreType.DMA((6,)),
-        pltpu.SemaphoreType.DMA((2, 2)),
+        pltpu.SemaphoreType.DMA((2, 3)),
         *[pltpu.VMEM((1, 1, 14, 14, D), BF16) for _ in range(4)],
         pltpu.VMEM((3, 4, 4, KV), F32),
-        pltpu.VMEM((2, CHUNK, D), BF16),
-        pltpu.VMEM((2, CHUNK, D), BF16),
+        pltpu.VMEM((3, CHUNK, D), BF16),
+        pltpu.VMEM((3, CHUNK, D), BF16),
         pltpu.VMEM((D, FIRST_COLS + LAST_COLS), BF16),
         pltpu.VMEM((HALF, MLP_COLS), BF16), *landing(MLP_COLS),
         *landing(FIRST_COLS),
         *landing(LAST_COLS),
         pltpu.VMEM((4, D, D), BF16),
-        pltpu.VMEM((3, D, D), BF16),
+        pltpu.VMEM((4, D, D), BF16),
         pltpu.VMEM((3, 16, KV), F32),
         pltpu.VMEM((14, 16, D), BF16),
         pltpu.VMEM((ROWS, D), BF16),
@@ -755,7 +752,7 @@
         pltpu.VMEM((2, 16, KV), BF16),
         pltpu.VMEM((ROWS, D), BF16),
         pltpu.VMEM((ROWS, D), BF16),
-        pltpu.VMEM((2, 128, KV), BF16),
+        pltpu.VMEM((48, KV), BF16),
         pltpu.VMEM((128, D), F32),
         pltpu.VMEM((6, 2, FF), F32),
         pltpu.VMEM((6, 4, D), F32),

time: 109 us -> 104 us (0.954); the launches traced: 108 us -> 104 us
  Pallas kernels: 107 us -> 103 us
    pallas_call x1, Pallas kernels: 103 us -> 99.8 us  [run_block(): pl.pallas_call(block_kernel, in_specs=[hbm, hbm, hbm, hbm, vmem, hbm, hbm...]
where the time goes in v5:
time: 104 us
  Pallas kernels  103 us (99%)
    pallas_call x1, Pallas kernels, run_block(): pl.pallas_call(block_kernel, in_specs=[hbm, hbm, hbm, hbm, vmem, hbm, hbm...  99.8 us
    pallas_call x1, Pallas kernels, hand_out(): pl.pallas_call(hand_out_kernel, in_specs=[hbm] * 6 + [vmem], out_specs=[h...  3.5 us

profile of v5, /device:TPU:1, one launch (start us, length us, event | category | flops | bytes accessed | tf_op | source)
XLA Modules:
  0.0 104.1 jit_solution(9731864981492137891)
XLA Ops:
  0.6 99.8 %reversible_block.1 = (bf16[1,1,14,14,768]{4,3,2,1,0:T(8,128)(2,1)}, bf16[1,1,14,14,768]{4,3,2,1,0:T(8,128)(2,1)}, bf16[1,1,14,14,768]{4,3,2,1,0:T(8,128)(2,1)},...) custom-call(bf16[1,1,14,14,768]{4,3,2,1,0:T(8,128)(2,1)} %one_hbm.1, ...), custom_call_target="tpu_custom_call" | custom-call | tf_op jit(solution)/shard_map/reversible_block/pallas_call | solution.py:762
  100.4 3.5 %hand_out.1 = (bf16[1,1,14,14,768]{4,3,2,1,0:T(8,128)(2,1)}, bf16[1,1,14,14,768]{4,3,2,1,0:T(8,128)(2,1)}, bf16[1,1,14,14,768]{4,3,2,1,0:T(8,128)(2,1)}, bf16[1,...) custom-call(bf16[1,1,14,14,768]{4,3,2,1,0:T(8,128)(2,1)} %get-tuple-, ...), custom_call_target="tpu_custom_call" | custom-call | tf_op jit(solution)/shard_map/hand_out/pallas_call | solution.py:818

commit v6 on v5

--- a/solution.py
+++ b/solution.py
@@ -80,30 +80,37 @@
     ref[0, 0] = values.reshape(14, 16, D)[:, 0:14, :]
 
 
-def cell_maps():
-    row = iota((ROWS, 48), 0)
-    across, down = (row & 15) + 1, (row >> 4) + 1
-    valid = across < 15
-    cell = (down & 3) * 4 + (across & 3)
-    lane = iota((ROWS, 48), 1)
-    cells = jnp.where(valid & ((lane & 15) == cell), 1.0, 0.0).astype(BF16)
-    row = iota((ROWS, 16), 0)
-    across, down = (row & 15) + 1, (row >> 4) + 1
-    block = (down >> 2) * 4 + (across >> 2)
-    blocks = jnp.where((across < 15) & (iota((ROWS, 16), 1) == block), 1.0, 0.0).astype(BF16)
-    return cells, blocks
-
-
-def spread_kernel(cells, flat):
+def spread_kernel(flat):
+    row, lane = iota((64, 48), 0), iota((64, 48), 1)
+    cell = (row >> 4) * 4 + (((row & 15) + 1) & 3)
+    cells = jnp.where(((row & 15) < 14) & ((lane & 15) == cell), 1.0, 0.0).astype(BF16)
     high = flat.astype(BF16)
     rest = flat - high.astype(F32)
     middle = rest.astype(BF16)
     low = (rest - middle.astype(F32)).astype(BF16)
-    return dot(cells, jnp.concatenate([high, middle, low], axis=0))
-
-
-def gather_rows(one_hot, values):
-    return dot_tn(one_hot, values.astype(BF16))
+    table = dot(cells, jnp.concatenate([high, middle, low], axis=0))
+    return [table[16 * i : 16 * i + 16] for i in range(4)]
+
+
+def spread_blocks(frame):
+    row, lane = iota((64, 16), 0), iota((64, 16), 1)
+    block = (row >> 4) * 4 + (((row & 15) + 1) >> 2)
+    blocks = jnp.where(((row & 15) < 14) & (lane == block), 1.0, 0.0).astype(BF16)
+    table = dot(blocks, frame)
+    return [table[16 * a : 16 * a + 16] for a in range(4)]
+
+
+def sum_columns(tables, group):
+    row, lane = iota((48, 192), 0), iota((48, 192), 1)
+    across = lane & 15
+    same = (row >> 2 == lane >> 4) & (across < 14) & (group(across + 1) == (row & 3))
+    pick = jnp.where(same, 1.0, 0.0).astype(BF16)
+    stacked = jnp.concatenate([table.astype(BF16) for table in tables], axis=0)
+    return dot(pick, stacked)
+
+
+def add_to(tables, at, value):
+    tables[at] = value if tables[at] is None else tables[at] + value
 
 
 class Links:
@@ -302,7 +309,7 @@
     keys, values, d_keys, d_values = take(4)
     x_keys, z_keys, x_values, z_values = take(4)
     key_sum, value_sum, pair_sum, pair_land, edge_land = take(5)
-    attended, d_query, extra, extra_gain = take(4)
+    attended, d_query, extra, extra_gain, d_proj = take(5)
     mlp_sums, attn_sums, rest_sums, out_sem = take(4)
 
     place = Place()
@@ -375,8 +382,7 @@
             for copy in weight_copies(k + 3):
                 copy.start()
 
-    for k, axes in enumerate(ORDERS):
-        orders[k] = permutation(axes)
+    orders[1] = permutation(ORDERS[1])
     one_copy.wait()
     unit, scale = norm_stats(load_padded(one_in, pad).astype(F32))
     normed[...] = (unit * gain_ref[0:1, :]).astype(BF16)
@@ -451,13 +457,19 @@
     attn_copy.wait()
     keyval[:, 0:D] = dot(normed_two[...], attn[1]).astype(BF16)
     keyval[:, D:] = dot(normed_two[...], attn[2]).astype(BF16)
-    cells, blocks = cell_maps()
     pool_copy.wait()
+    sums = [None] * 12
     for offset in range(3):
         for i in range(4):
             pool[offset, 4 * i : 4 * i + 4, :] = pool_in[offset, i]
-        weighted = spread_kernel(cells, pool[offset]) * keyval[...].astype(F32)
-        parts[2 - offset] = gather_rows(blocks, weighted).astype(BF16)
+        table = spread_kernel(pool[offset])
+        for y_at in range(14):
+            row = keyval[16 * y_at : 16 * y_at + 16, :].astype(F32)
+            at = (2 - offset) * 4 + (y_at + 1) // 4
+            add_to(sums, at, table[(y_at + 1) % 4] * row)
+    pooled_parts = sum_columns(sums, lambda across: across >> 2).astype(BF16)
+    for k in range(3):
+        parts[k] = pooled_parts[16 * k : 16 * k + 16]
 
     mine = pl.ds(1 - low, 2)
     pl.semaphore_wait(barrier, len(partners))
@@ -473,6 +485,8 @@
     cot_two_copy.wait()
     cot[...] = load_padded(cot_two_in, pad)
     back(0)
+    orders[3] = permutation(ORDERS[3])
+    orders[0] = permutation(ORDERS[0])
     pair_copy.wait_recv()
     for slot in range(2):
         links.arrival(from_edge.at[slot], edge_base + slot)
@@ -489,6 +503,7 @@
         copies.append(links.start(keys.at[x, z], keys.at[x, z], place.along(2, hop)[0]))
         copies.append(links.start(values.at[x, z], values.at[x, z], place.along(0, hop)[0]))
     back(1)
+    orders[2] = permutation(ORDERS[2])
     for copy in copies:
         copy.wait_recv()
     copies = []
@@ -632,16 +647,20 @@
     here = jnp.where(low == 0, frame_0, frame_1)
     after = jnp.where(low == 0, frame_1, edge)
 
-    cells, blocks = cell_maps()
-    keyval_f = keyval[...].astype(F32)
-    d_keyval = None
+    sums = [None] * 12
+    d_rows = [None] * 14
     for offset, source in enumerate((after, here, before)):
-        expanded = dot(blocks, source)
-        term = spread_kernel(cells, pool[offset]) * expanded
-        d_keyval = term if d_keyval is None else d_keyval + term
-        d_kernel = gather_rows(cells[:, 0:16], keyval_f * expanded).astype(BF16)
-        extra[16 * offset : 16 * offset + 16, :] = d_kernel
-    d_keyval = d_keyval.astype(BF16)
+        table = spread_kernel(pool[offset])
+        expanded = spread_blocks(source)
+        for y_at in range(14):
+            i, block = (y_at + 1) % 4, (y_at + 1) // 4
+            row = keyval[16 * y_at : 16 * y_at + 16, :].astype(F32)
+            add_to(d_rows, y_at, table[i] * expanded[block])
+            add_to(sums, offset * 4 + i, row * expanded[block])
+    extra[...] = sum_columns(sums, lambda across: across & 3).astype(BF16)
+    for y_at in range(14):
+        d_proj[16 * y_at : 16 * y_at + 16, :] = d_rows[y_at].astype(BF16)
+    d_keyval = d_proj[...]
     d_key_proj, d_value_proj = d_keyval[:, 0:D], d_keyval[:, D:]
 
     def last_part(part):
@@ -656,6 +675,7 @@
         last_part(part)
         last.send0(part)
     last_part(2)
+    last.send1(0)
     d_normed_two = branch[...] + dot_nt(d_key_proj, attn[1]) + dot_nt(d_value_proj, attn[2])
     row, lane = iota((256, 256), 0), iota((256, 256), 1)
     parted = jnp.where(row == 2 * (lane & 127) + (lane >> 7), 1.0, 0.0).astype(BF16)
@@ -670,7 +690,6 @@
     block = dot_nt(orders[2], extra_gain[...].astype(BF16))
     stage[:, pl.ds(FIRST_COLS + 1536, 128)] = block.astype(BF16)
     last.send0(2)
-    last.send1(0)
     last.send1(1)
     d_second = norm_back(unit_two, scale_two, gain_ref[1:2, :], d_normed_two)
     result = load_padded(cot_two_in, pad).astype(F32) + d_second
@@ -754,6 +773,7 @@
         pltpu.VMEM((ROWS, D), BF16),
         pltpu.VMEM((48, KV), BF16),
         pltpu.VMEM((128, D), F32),
+        pltpu.VMEM((ROWS, KV), BF16),
         pltpu.VMEM((6, 2, FF), F32),
         pltpu.VMEM((6, 4, D), F32),
         pltpu.VMEM((8, 128), F32),

time: 104 us -> 103 us (level)
    pallas_call x1, Pallas kernels: 99.8 us -> 98.7 us  [run_block(): pl.pallas_call(block_kernel, in_specs=[hbm, hbm, hbm, hbm, vmem, hbm, hbm...]
where the time goes in v6:
time: 103 us
  Pallas kernels  102 us (99%)
    pallas_call x1, Pallas kernels, run_block(): pl.pallas_call(block_kernel, in_specs=[hbm, hbm, hbm, hbm, vmem, hbm, hbm...  98.7 us
    pallas_call x1, Pallas kernels, hand_out(): pl.pallas_call(hand_out_kernel, in_specs=[hbm] * 6 + [vmem], out_specs=[h...  3.5 us

profile of v6, /device:TPU:1, one launch (start us, length us, event | category | flops | bytes accessed | tf_op | source)
XLA Modules:
  0.0 103.0 jit_solution(4677394428301135102)
XLA Ops:
  0.6 98.7 %reversible_block.1 = (bf16[1,1,14,14,768]{4,3,2,1,0:T(8,128)(2,1)}, bf16[1,1,14,14,768]{4,3,2,1,0:T(8,128)(2,1)}, bf16[1,1,14,14,768]{4,3,2,1,0:T(8,128)(2,1)},...) custom-call(bf16[1,1,14,14,768]{4,3,2,1,0:T(8,128)(2,1)} %one_hbm.1, ...), custom_call_target="tpu_custom_call" | custom-call | tf_op jit(solution)/shard_map/reversible_block/pallas_call | solution.py:782
  99.3 3.5 %hand_out.1 = (bf16[1,1,14,14,768]{4,3,2,1,0:T(8,128)(2,1)}, bf16[1,1,14,14,768]{4,3,2,1,0:T(8,128)(2,1)}, bf16[1,1,14,14,768]{4,3,2,1,0:T(8,128)(2,1)}, bf16[1,...) custom-call(bf16[1,1,14,14,768]{4,3,2,1,0:T(8,128)(2,1)} %get-tuple-, ...), custom_call_target="tpu_custom_call" | custom-call | tf_op jit(solution)/shard_map/hand_out/pallas_call | solution.py:838

commit v7 on v6

--- a/solution.py
+++ b/solution.py
@@ -215,14 +215,14 @@
         first, count = self.parts[part]
 
         def body(k, carry):
-            rows = pl.ds(pl.multiple_of(k * 16, 16), 16)
-            mine = pl.ds(pl.multiple_of(self.base + k * 16, 16), 16)
+            rows = pl.ds(pl.multiple_of(k * 48, 48), 48)
+            mine = pl.ds(pl.multiple_of(self.base + k * 48, 48), 48)
             cols, held_cols = pl.ds(first, count), pl.ds(first + self.offset, count)
             total = self.held[mine, held_cols].astype(F32) + self.in0[rows, cols].astype(F32)
             self.held[mine, held_cols] = total.astype(BF16)
             return carry
 
-        lax.fori_loop(0, HALF // 16, body, 0)
+        lax.fori_loop(0, HALF // 48, body, 0)
         self.spread(1, part, self.held, self.base, self.offset, 96, self.in1)
 
     def send2(self, part):

time: 103 us -> 102 us (level)
  no operation moved by 1% of the time
where the time goes in v7:
time: 102 us
  Pallas kernels  101 us (99%)
    pallas_call x1, Pallas kernels, run_block(): pl.pallas_call(block_kernel, in_specs=[hbm, hbm, hbm, hbm, vmem, hbm, hbm...  97.8 us
    pallas_call x1, Pallas kernels, hand_out(): pl.pallas_call(hand_out_kernel, in_specs=[hbm] * 6 + [vmem], out_specs=[h...  3.5 us

profile of v7, /device:TPU:1, one launch (start us, length us, event | category | flops | bytes accessed | tf_op | source)
XLA Modules:
  0.0 102.1 jit_solution(18105609502075230249)
XLA Ops:
  0.6 97.8 %reversible_block.1 = (bf16[1,1,14,14,768]{4,3,2,1,0:T(8,128)(2,1)}, bf16[1,1,14,14,768]{4,3,2,1,0:T(8,128)(2,1)}, bf16[1,1,14,14,768]{4,3,2,1,0:T(8,128)(2,1)},...) custom-call(bf16[1,1,14,14,768]{4,3,2,1,0:T(8,128)(2,1)} %one_hbm.1, ...), custom_call_target="tpu_custom_call" | custom-call | tf_op jit(solution)/shard_map/reversible_block/pallas_call | solution.py:782
  98.4 3.5 %hand_out.1 = (bf16[1,1,14,14,768]{4,3,2,1,0:T(8,128)(2,1)}, bf16[1,1,14,14,768]{4,3,2,1,0:T(8,128)(2,1)}, bf16[1,1,14,14,768]{4,3,2,1,0:T(8,128)(2,1)}, bf16[1,...) custom-call(bf16[1,1,14,14,768]{4,3,2,1,0:T(8,128)(2,1)} %get-tuple-, ...), custom_call_target="tpu_custom_call" | custom-call | tf_op jit(solution)/shard_map/hand_out/pallas_call | solution.py:838
